TPU v7x, 256 devices: a whole 4x4x8 slice. The times are simulated.
256 devices in a mesh: ctx: 32 (over x, z), head: 8 (over y, core).
Axes of the slice: x: 4, y: 4, z: 8, core: 2. Of those that a mesh axis runs over, the one named last changes fastest.
Arguments:
- x_in: bfloat16 [32768, 16384], P('ctx', 'head'), may hold values from -6 to 6
- bc_in: bfloat16 [32768, 2, 1024], P(('ctx', 'head')), may hold values from -6 to 6
- z_in: bfloat16 [32768, 16384], P('ctx', 'head'), may hold values from -6 to 6
- dt: float32 [32768, 256], P('ctx', 'head'), may hold values from 0.001 to 0.1
- log_decay: float32 [32768, 256], P('ctx', 'head'), may hold values from -1 to 0
- x_kernel: float32 [4, 16384], P(None, 'head'), may hold values from -3 to 3
- bc_kernel: float32 [4, 2, 1024], P(None, None, 'head'), may hold values from -3 to 3
- x_bias: float32 [16384], P('head'), may hold values from -1 to 0
- bc_bias: float32 [2, 1024], P(None, 'head'), may hold values from -1 to 0
- skip: float32 [256], P('head'), may hold values from 0.5 to 1.5
- norm_gain: float32 [16384], P('head'), may hold values from 0.5 to 1.5
Outputs:
- mixed: bfloat16 [32768, 16384], P('ctx', 'head')
All inputs are finite; a program needn't handle non-finite values.
Results may differ from a plain program's by a relative error of at most 0.012.
Values may be sent and summed in bfloat16 or wider, within the bound.
A program may use at most 128 MiB of HBM per device.

v0:
```python
import jax
import jax.numpy as jnp
from jax import lax
from jax.sharding import PartitionSpec as P

HEAD_DIM = 64
STATE = 128
KERNEL = 4
BLOCK_LENGTH = 512


def from_behind(block, axis, distance):
    devices = range(lax.axis_size(axis))
    route = [(i - distance, i) for i in devices if i - distance in devices]
    return lax.ppermute(block, axis, route)


def carried_in(part, axis, combine, identity):
    place = lax.axis_index(axis)
    gathered = jax.tree.map(lambda a: lax.all_gather(a, axis), part)
    state = jax.tree.map(lambda a, e: jnp.zeros_like(a) + jnp.asarray(e, a.dtype), part, identity)

    def one(hop, state):
        return combine(
            state, jax.tree.map(lambda a: lax.dynamic_index_in_dim(a, hop, 0, False), gathered)
        )

    return lax.fori_loop(0, place, one, state)


def conv_silu(seq, rim, kernel, bias):
    padded = jnp.concatenate([rim, seq], axis=0).astype(jnp.float32)
    length = seq.shape[0]
    total = jnp.broadcast_to(bias, seq.shape)
    for tap in range(KERNEL):
        total = total + kernel[tap] * padded[tap : tap + length]
    return jax.nn.silu(total).astype(jnp.bfloat16)


def compose(earlier, later):
    return (earlier[0] * later[0], earlier[1] * later[0][:, None, None] + later[1])


def per_device(
    x_in, bc_in, z_in, dt, log_decay, x_kernel, bc_kernel, x_bias, bc_bias, skip, norm_gain
):
    bc_local = lax.all_to_all(bc_in, "head", split_axis=2, concat_axis=0, tiled=True)
    edge = KERNEL - 1
    rim_x, rim_bc = from_behind((x_in[-edge:], bc_local[-edge:]), "ctx", 1)
    xc = conv_silu(x_in, rim_x, x_kernel, x_bias)
    bcc = conv_silu(bc_local, rim_bc, bc_kernel, bc_bias)
    rows = x_in.shape[0]
    heads_here = x_in.shape[1] // HEAD_DIM
    groups_here = bc_local.shape[2] // STATE
    heads_per_group = heads_here // groups_here
    places = jnp.arange(BLOCK_LENGTH)
    causal = (places[:, None] >= places[None, :])[None]
    local_state = jnp.zeros((heads_here, HEAD_DIM, STATE), jnp.float32)
    dev_decay = jnp.ones((heads_here,), jnp.float32)
    base_parts, c_parts, before_states, preceding_attenuation = ([], [], [], [])
    for block in range(rows // BLOCK_LENGTH):
        lower = block * BLOCK_LENGTH
        xb = xc[lower : lower + BLOCK_LENGTH].reshape(BLOCK_LENGTH, heads_here, HEAD_DIM)
        bb = bcc[lower : lower + BLOCK_LENGTH, 0].reshape(BLOCK_LENGTH, groups_here, STATE)
        cb = bcc[lower : lower + BLOCK_LENGTH, 1].reshape(BLOCK_LENGTH, groups_here, STATE)
        db = dt[lower : lower + BLOCK_LENGTH]
        cum = jnp.cumsum(log_decay[lower : lower + BLOCK_LENGTH], axis=0)
        scores = jnp.einsum("tgn,sgn->gts", cb, bb, preferred_element_type=jnp.float32)
        scores = jnp.repeat(scores, heads_per_group, axis=0)
        cum_h = cum.T
        gap = jnp.where(causal, cum_h[:, :, None] - cum_h[:, None, :], 0.0)
        mix = jnp.where(causal, scores * jnp.exp(gap) * db.T[:, None, :], 0.0).astype(jnp.bfloat16)
        y_intra = jnp.einsum("hts,shp->thp", mix, xb, preferred_element_type=jnp.float32)
        last = cum[-1]
        weight = jnp.exp(last[None, :] - cum) * db
        b_heads = jnp.repeat(bb, heads_per_group, axis=1).astype(jnp.float32)
        b_w = (b_heads * weight[:, :, None]).astype(jnp.bfloat16)
        fresh = jnp.einsum("thn,thp->hpn", b_w, xb, preferred_element_type=jnp.float32)
        c_heads = jnp.repeat(cb, heads_per_group, axis=1).astype(jnp.float32)
        c_parts.append((c_heads * jnp.exp(cum)[:, :, None]).astype(jnp.bfloat16))
        base_parts.append(y_intra + skip[None, :, None] * xb.astype(jnp.float32))
        before_states.append(local_state)
        preceding_attenuation.append(dev_decay)
        local_state = local_state * jnp.exp(last)[:, None, None] + fresh
        dev_decay = dev_decay * jnp.exp(last)
    identity = (
        jnp.ones((heads_here,), jnp.float32),
        jnp.zeros((heads_here, HEAD_DIM, STATE), jnp.float32),
    )
    prefix = carried_in((dev_decay, local_state), "ctx", compose, identity)
    entering = prefix[1]
    outputs = []
    for block in range(rows // BLOCK_LENGTH):
        full = before_states[block] + entering * preceding_attenuation[block][:, None, None]
        y_inter = jnp.einsum(
            "thn,hpn->thp",
            c_parts[block],
            full.astype(jnp.bfloat16),
            preferred_element_type=jnp.float32,
        )
        outputs.append(base_parts[block] + y_inter)
    y = jnp.concatenate(outputs, axis=0).reshape(rows, heads_here * HEAD_DIM)
    gated = y * jax.nn.silu(z_in.astype(jnp.float32))
    grouped = gated.reshape(rows, groups_here, -1)
    scale = lax.rsqrt(jnp.mean(grouped * grouped, axis=-1, keepdims=True) + 1e-05)
    normed = (grouped * scale).reshape(rows, heads_here * HEAD_DIM) * norm_gain
    return normed.astype(jnp.bfloat16)


def solution(mesh):
    placed = (
        P("ctx", "head"),
        P(("ctx", "head"), None, None),
        P("ctx", "head"),
        P("ctx", "head"),
        P("ctx", "head"),
        P(None, "head"),
        P(None, None, "head"),
        P("head"),
        P(None, "head"),
        P("head"),
        P("head"),
    )
    return jax.shard_map(
        per_device, mesh=mesh, in_specs=placed, out_specs=P("ctx", "head"), check_vma=False
    )
```

profile of v0, /device:TPU:230, one launch (start us, length us, event | category | flops | bytes accessed | tf_op | source)
XLA Modules:
  0.0 382.7 jit_solution(10697685980814745509)
XLA Ops:
  7.3 1.3 collective-permute-start
  8.6 3.0 copy.34
  11.6 4.5 %all-to-all-start = ((bf16[128,2,1024]{0,1,2:T(2,128)(2,1)}), bf16[128,2,1024]{0,1,2:T(2,128)(2,1)S(1)}, u32[]{:S(2)}, u32[]{:S(2)}) async-start(bf16[128,2,1024]{0,1,2:T(2,128)(2,1)} %copy.34), calls=%async_computation | async-start | bytes 1048576 | tf_op jit(solution)/shard_map/all_to_all | solution.py:47
  16.9 0.9 fusion.43
  17.8 0.9 slice_bitcast_fusion.9
  18.7 1.2 reduce-window.16
  20.1 1.2 reduce-window.14
  23.6 1.7 slice_bitcast_fusion.11
  25.9 3.4 maximum_convert_fusion
  29.3 6.7 %multiply_convert_fusion.5 = bf16[1024,2048]{1,0:T(8,128)(2,1)} fusion(f32[1027,2048]{1,0:T(8,128)S(1)} %maximum_convert_fusion, f32[2048]{0:T(1024)S(1)} %bitcast.125, f32[2048]{0:T(1024)S(1)} %bitcast.126, f32[2048]{0:T(1024)S(1)} %bitcast.124, f32[2048]{0:T(1024)S(1)} %bitcast.123, f32[2048]{0:T(1024)S(1)} %copy-done.10), kind=kLoop, calls=%fused_computation.29 | loop fusion | flops 27262976 | bytes 37789696 | tf_op jit(solution)/shard_map/convert_element_type | solution.py:37
  36.4 0.8 copy-done.4
  37.1 1.4 collective-permute-start.1
  38.6 4.0 %fusion.42 = (bf16[512,2048]{1,0:T(8,128)(2,1)S(1)}, bf16[512,2048]{1,0:T(8,128)(2,1)}) fusion(bf16[1024,2048]{1,0:T(8,128)(2,1)} %multiply_convert_fusion.5), kind=kLoop, calls=%fused_computation.102 | loop fusion | bytes 8388608 | tf_op jit(solution)/shard_map/slice | solution.py:63
  42.6 2.5 copy.33
  45.1 2.9 copy.41
  47.9 1.2 maximum_convert_fusion.1
  49.8 0.8 fusion.32
  50.6 4.5 %fusion.25 = f32[32,64,128]{2,1,0:T(8,128)S(1)} fusion(bf16[512,32,64]{0,2,1:T(8,128)(2,1)} %bitcast.116, f32[512,32]{0,1:T(8,128)} %get-tuple-element.70, f32[512,128]{1,0:T(8,128)S(1)} %get-tuple-element.68, f32[32]{0:T(128)S(1)} %get-tuple-element.90), kind=kOutput, calls=%fused_computation.48 | convolution fusion | flops 272891904 | bytes 3473536 | tf_op jit(solution)/shard_map/thn,thp->hpn/dot_general | solution.py:78
  55.2 1.0 copy-done.5
  56.1 3.9 %fusion.24 = f32[32,64,128]{2,1,0:T(8,128)} fusion(bf16[512,32,64]{0,2,1:T(8,128)(2,1)S(1)} %bitcast.113, f32[512,32]{0,1:T(8,128)S(1)} %copy-done.9, f32[512,128]{1,0:T(8,128)S(1)} %get-tuple-element.67, f32[32,64,128]{2,1,0:T(8,128)S(1)} %fusion.25, f32[32]{0:T(128)S(1)} %exp.58), kind=kOutput, calls=%fused_computation.47 | convolution fusion | flops 273154048 | bytes 4522112 | tf_op jit(solution)/shard_map/thn,thp->hpn/dot_general | solution.py:78
  60.1 38.7 %all-gather.1 = f32[32,1,32]{2,1,0:T(1,128)S(1)} all-gather(f32[1,1,32]{2,1,0:T(1,128)} %bitcast.128), channel_id=1, replica_groups=mesh['ctx'=32,'head'=8] {'ctx'}, dimensions={0}, use_global_device_ids=true | all-gather | bytes 4224 | tf_op jit(solution)/shard_map/all_gather | solution.py:20
  99.5 11.7 %fusion.1 = f32[32,64,512]{2,1,0:T(8,128)} fusion(bf16[512,32,64]{0,2,1:T(8,128)(2,1)S(1)} %bitcast.114, f32[32,512]{1,0:T(8,128)} %get-tuple-element.71, f32[32,512]{1,0:T(8,128)} %get-tuple-element.80, f32[512,512]{1,0:T(8,128)S(1)} %fusion.35, pred[512,512]{1,0:T(8,128)(4,1)S(1)} %iota_compare_fusion), kind=kOutput, calls=%fused_computation.5 | convolution fusion | flops 1124073472 | bytes 7733248 | tf_op jit(solution)/shard_map/hts,shp->thp/dot_general | solution.py:73
  111.2 10.9 %fusion = f32[32,64,512]{2,1,0:T(8,128)} fusion(bf16[512,32,64]{0,2,1:T(8,128)(2,1)S(1)} %bitcast.118, f32[32,512]{1,0:T(8,128)S(1)} %copy-done.8, f32[32,512]{1,0:T(8,128)S(1)} %copy-done.7, f32[512,512]{1,0:T(8,128)S(1)} %fusion.33, pred[512,512]{1,0:T(8,128)(4,1)S(1)} %iota_compare_fusion), kind=kOutput, calls=%fused_computation.4 | convolution fusion | flops 1124073472 | bytes 7733248 | tf_op jit(solution)/shard_map/hts,shp->thp/dot_general | solution.py:73
  122.1 171.5 %all-gather.4.cloned.1.call-done = f32[1024,64,128]{2,1,0:T(8,128)} async-done(((f32[32,64,128]{2,1,0:T(8,128)}), f32[1024,64,128]{2,1,0:T(8,128)}) %all-gather.4.cloned.1.call-update) | async-done | bytes 33554448 | tf_op jit(solution)/shard_map/all_gather | solution.py:20
  293.7 46.5 %while.12 = (s32[]{:T(128)}, f32[32,64,128]{2,1,0:T(8,128)S(1)}, s32[]{:T(128)}, f32[32,32]{1,0:T(8,128)S(1)}, f32[32,32,64,128]{3,2,1,0:T(8,128)}, /*index=5*/s32[]{:T(128)}, s32[]{:T(128)}, s32[]{:T(128)}) while((s32[]{:T(128)}, f32[32,64,128]{2,1,0:T(8,128)S(1)}, s32[]{:T(128)}, f32[32,32]{1,0:T(8,128)S(1)}, f32[32,32,64,128]{3,2,1,0:T(8,128)}, ...), condition=%wide.region_5.6_spmd, body=%wide.region_4.5_spmd.sunk | while | flops 524293 | bytes 3146247 | solution.py:28
  293.8 1.4 bitcast_add_fusion.6
  295.3 1.4 bitcast_add_fusion.6
  296.8 1.4 bitcast_add_fusion.6
  298.2 1.4 bitcast_add_fusion.6
  299.7 1.4 bitcast_add_fusion.6
  301.2 1.4 bitcast_add_fusion.6
  302.7 1.4 bitcast_add_fusion.6
  304.2 1.4 bitcast_add_fusion.6
  305.7 1.4 bitcast_add_fusion.6
  307.2 1.4 bitcast_add_fusion.6
  308.7 1.4 bitcast_add_fusion.6
  310.2 1.4 bitcast_add_fusion.6
  311.7 1.4 bitcast_add_fusion.6
  313.2 1.4 bitcast_add_fusion.6
  314.7 1.4 bitcast_add_fusion.6
  316.1 1.4 bitcast_add_fusion.6
  317.6 1.4 bitcast_add_fusion.6
  319.1 1.4 bitcast_add_fusion.6
  320.6 1.4 bitcast_add_fusion.6
  322.1 1.4 bitcast_add_fusion.6
  323.6 1.4 bitcast_add_fusion.6
  325.1 1.4 bitcast_add_fusion.6
  326.6 1.4 bitcast_add_fusion.6
  328.1 1.4 bitcast_add_fusion.6
  329.6 1.4 bitcast_add_fusion.6
  331.1 1.4 bitcast_add_fusion.6
  332.6 1.4 bitcast_add_fusion.6
  334.0 1.4 bitcast_add_fusion.6
  335.5 1.4 bitcast_add_fusion.6
  337.0 1.4 bitcast_add_fusion.6
  338.5 1.4 bitcast_add_fusion.6
  340.2 5.6 %bitcast_add_fusion.3 = f32[512,32,64]{0,2,1:T(8,128)S(1)} fusion(f32[32,64,512]{2,1,0:T(8,128)} %fusion, bf16[512,32,64]{0,2,1:T(8,128)(2,1)} %bitcast.117, f32[512,32]{0,1:T(8,128)S(1)} %get-tuple-element.76, f32[512,128]{1,0:T(8,128)} %get-tuple-element.65, f32[32]{0:T(128)} %param.22, f32[32,64,128]{2,1,0:T(8,128)S(1)} %get-tuple-element.49), kind=kOutput, calls=%fused_computation.37 | convolution fusion | flops 277086208 | bytes 11862144 | tf_op jit(solution)/shard_map/thn,hpn->thp/dot_general | solution.py:95
  345.9 2.7 bitcast_add_fusion.1
  348.7 4.5 %pad_maximum_fusion = f32[1024,32,64]{0,2,1:T(8,128)} fusion(f32[512,32,64]{0,2,1:T(8,128)S(1)} %bitcast_add_fusion.1, f32[512,32,64]{0,2,1:T(8,128)S(1)} %bitcast_add_fusion.3), kind=kLoop, calls=%fused_computation.22 | loop fusion | flops 2097152 | bytes 16777216 | tf_op jit(solution)/shard_map/concatenate | solution.py:102
  353.1 9.2 %copy.42 = f32[1024,2048]{1,0:T(8,128)} copy(f32[1024,2048]{0,1:T(8,128)} %bitcast.112) | data formatting | bytes 16777216 | tf_op jit(solution)/shard_map/reshape | solution.py:102
  362.3 6.2 %multiply_reduce_fusion = f32[1024]{0:T(1024)S(1)} fusion(f32[1024,2048]{1,0:T(8,128)} %copy.42, bf16[1024,2048]{1,0:T(8,128)(2,1)} %param.15), kind=kLoop, calls=%fused_computation.24 | loop fusion | flops 16776192 | bytes 12587008 | tf_op jit(solution)/shard_map/reduce_sum | solution.py:105
  368.5 0.8 copy-done
  369.4 1.2 copy-done.1
  370.6 5.3 %multiply_convert_fusion = bf16[1024,2048]{1,0:T(8,128)(2,1)} fusion(f32[2048]{0:T(1024)S(1)} %copy-done.11, f32[1024]{0:T(1024)S(1)} %add_rsqrt_fusion, f32[1024,2048]{1,0:T(8,128)S(1)} %copy-done, bf16[1024,2048]{1,0:T(8,128)(2,1)S(1)} %copy-done.1), kind=kLoop, calls=%fused_computation.23 | loop fusion | flops 18874368 | bytes 16789504 | tf_op jit(solution)/shard_map/convert_element_type | solution.py:107
  (85 shorter events, 6.9 us)
Async XLA Ops:
  7.3 22.0 %copy-start.10 = (f32[2048]{0:T(1024)S(1)}, f32[2048]{0:T(1024)}, u32[]{:S(2)}) copy-start(f32[2048]{0:T(1024)} %param.20) | copy-start | bytes 24580
  7.3 18.6 %collective-permute-start = (bf16[3,2048]{1,0:T(4,128)(2,1)S(1)}, bf16[3,2048]{1,0:T(4,128)(2,1)S(1)}, u32[]{:S(2)}, u32[]{:S(2)}) collective-permute-start(bf16[3,2048]{1,0:T(4,128)(2,1)S(1)} %slice.105), channel_id=1, source_target_pairs={{0,8},{8,16},{16,24},{24,32},{32,40},{40,48},{48,56},{56,64},{64,7... | collective-permute-start | bytes 36872 | tf_op jit(solution)/shard_map/ppermute | solution.py:15
  11.6 24.4 %all-to-all-start = ((bf16[128,2,1024]{0,1,2:T(2,128)(2,1)}), bf16[128,2,1024]{0,1,2:T(2,128)(2,1)S(1)}, u32[]{:S(2)}, u32[]{:S(2)}) async-start(bf16[128,2,1024]{0,1,2:T(2,128)(2,1)} %copy.34), calls=%async_computation | async-start | bytes 1048576 | tf_op jit(solution)/shard_map/all_to_all | solution.py:47
  16.1 277.5 %all-gather.4.cloned.1.call-start = ((), (), s32[]{:S(2)}) async-start(), calls=%async_computation.1 | async-start | bytes 34603008 | tf_op jit(solution)/shard_map/all_gather | solution.py:20
  36.3 0.8 copy-start.4
  37.1 12.0 %copy-start.13 = (f32[2,128]{1,0:T(2,128)S(1)}, f32[2,128]{1,0:T(2,128)}, u32[]{:S(2)}) copy-start(f32[2,128]{1,0:T(2,128)} %param.21) | copy-start | bytes 3076
  37.1 10.8 %collective-permute-start.1 = (bf16[3,2,128]{2,0,1:T(4,128)(2,1)S(1)}, bf16[3,2,128]{2,0,1:T(4,128)(2,1)S(1)}, u32[]{:S(2)}, u32[]{:S(2)}) collective-permute-start(bf16[3,2,128]{2,0,1:T(4,128)(2,1)S(1)} %slice.144), channel_id=1, source_target_pairs={{0,8},{8,16},{16,24},{24,32},{32,40},{40,48},{48,56},{56,64},{64,7... | collective-permute-start | bytes 4616 | tf_op jit(solution)/shard_map/ppermute | solution.py:15
  47.9 8.2 %copy-start.9 = (f32[512,32]{0,1:T(8,128)S(1)}, f32[512,32]{0,1:T(8,128)}, u32[]{:S(2)}) copy-start(f32[512,32]{0,1:T(8,128)} %get-tuple-element.72) | copy-start | bytes 196612
  55.1 1.0 copy-start.5
  99.5 11.8 %copy-start.2 = (bf16[512,2048]{0,1:T(8,128)(2,1)S(1)}, bf16[512,2048]{0,1:T(8,128)(2,1)}, u32[]{:S(2)}) copy-start(bf16[512,2048]{0,1:T(8,128)(2,1)} %copy.33) | copy-start | bytes 6291460
  99.5 11.8 %copy-start.7 = (f32[32,512]{1,0:T(8,128)S(1)}, f32[32,512]{1,0:T(8,128)}, u32[]{:S(2)}) copy-start(f32[32,512]{1,0:T(8,128)} %get-tuple-element.77) | copy-start | bytes 196612
  99.5 11.8 %copy-start.8 = (f32[32,512]{1,0:T(8,128)S(1)}, f32[32,512]{1,0:T(8,128)}, u32[]{:S(2)}) copy-start(f32[32,512]{1,0:T(8,128)} %get-tuple-element.69) | copy-start | bytes 196612
  340.2 5.7 %copy-start.3 = (f32[32,64,512]{2,1,0:T(8,128)S(1)}, f32[32,64,512]{2,1,0:T(8,128)}, u32[]{:S(2)}) copy-start(f32[32,64,512]{2,1,0:T(8,128)} %fusion.1) | copy-start | bytes 12582916
  340.2 5.7 %copy-start.6 = (f32[32,64,128]{2,1,0:T(8,128)S(1)}, f32[32,64,128]{2,1,0:T(8,128)}, u32[]{:S(2)}) copy-start(f32[32,64,128]{2,1,0:T(8,128)} %copy-done.5) | copy-start | bytes 3145732
  340.2 5.7 %copy-start.12 = (f32[32]{0:T(128)S(1)}, f32[32]{0:T(128)}, u32[]{:S(2)}) copy-start(f32[32]{0:T(128)} %param.22) | copy-start | bytes 388
  340.2 5.7 %copy-start.14 = (f32[32]{0:T(128)S(1)}, f32[32]{0:T(128)}, u32[]{:S(2)}) copy-start(f32[32]{0:T(128)} %get-tuple-element.89) | copy-start | bytes 388
  362.3 7.0 %copy-start = (f32[1024,2048]{1,0:T(8,128)S(1)}, f32[1024,2048]{1,0:T(8,128)}, u32[]{:S(2)}) copy-start(f32[1024,2048]{1,0:T(8,128)} %copy.42) | copy-start | bytes 25165828
  362.3 8.2 %copy-start.1 = (bf16[1024,2048]{1,0:T(8,128)(2,1)S(1)}, bf16[1024,2048]{1,0:T(8,128)(2,1)}, u32[]{:S(2)}) copy-start(bf16[1024,2048]{1,0:T(8,128)(2,1)} %param.15) | copy-start | bytes 12582916
  362.3 8.2 %copy-start.11 = (f32[2048]{0:T(1024)S(1)}, f32[2048]{0:T(1024)}, u32[]{:S(2)}) copy-start(f32[2048]{0:T(1024)} %param.23) | copy-start | bytes 24580
Sparse Core Ops, SparseCore 0:
  60.2 233.3 all-gather.3
where the time goes:
time: 385 us; the launch traced here: 383 us
  waiting for transfers between devices  172 us (45%)
  other arithmetic  80.4 us (21%)
  matrix products  40 us (10%)
  blocking collectives  38.7 us (10%)
  local copies, waits for them, and re-layouts  29.9 us (8%)
  between operations  13.7 us (4%)
  starting transfers between devices  7.21 us (2%)
    all_gather x1, waiting for transfers between devices, carried_in(): gathered = jax.tree.map(lambda a: lax.all_gather(a, axis), part)  171 us
    add x31, other arithmetic, compose(): earlier[1] * later[0][:, None, None] + later[1]  44.9 us
    all_gather x1, blocking collectives, carried_in(): gathered = jax.tree.map(lambda a: lax.all_gather(a, axis), part)  38.7 us
    dot_general x2, matrix products, per_device(): jnp.einsum('hts,shp->thp', mix, xb, preferred_element_type=jnp.float32)  22.6 us
    slice x3, local copies, waits for them, and re-layouts, per_device(): xc[lower:lower + BLOCK_LENGTH].reshape(BLOCK_LENGTH, heads_here, HEAD_DIM)  9.35 us
    reshape x1, local copies, waits for them, and re-layouts, per_device(): y = jnp.concatenate(outputs, axis=0).reshape(rows, heads_here * HEAD_DIM)  9.19 us
    dot_general x2, matrix products, per_device(): jnp.einsum('thn,thp->hpn', b_w, xb, preferred_element_type=jnp.float32)  8.44 us
    dot_general x2, matrix products, per_device(): jnp.einsum('thn,hpn->thp', c_parts[block], full.astype(jnp.bfloat16), pre...  8.37 us
  transfers between devices with their start and end apart: 4, of which 1 were waited for; matrix products, arithmetic and copies ran while one was open for 14% of the time, Pallas kernels for 0%

commit v1 on v0

v1 whole, which is shorter than its diff:
```python
import functools

import jax
import jax.numpy as jnp
from jax import lax
from jax.experimental import pallas as pl
from jax.experimental.pallas import tpu as pltpu
from jax.sharding import PartitionSpec as P

MESH = pl.DeviceIdType.MESH
F32, BF16 = jnp.float32, jnp.bfloat16
HEAD_DIM = 64
STATE = 128
CHUNK = 128
HALO = 16
WIDE = 256
HIGHEST = lax.Precision.HIGHEST


def split(value):
    high = value.astype(BF16)
    low = (value - high.astype(F32)).astype(BF16)
    return jnp.concatenate([high, low], axis=0)


def across(left, right):
    return lax.dot_general(left, right, (((0,), (0,)), ((), ())), preferred_element_type=F32)


def dot(left, right):
    return jnp.dot(left, right, preferred_element_type=F32)


def swish_of_twice(half):
    return half + half * jnp.tanh(half)


def kernel(
    sizes,
    x_hbm, bc_hbm, z_hbm, dt_ref, decay_ref, xk_ref, bck_ref, xb_ref, bcb_ref, skip_ref, gain_ref,
    out_hbm,
    x_buf, xc_buf, xs_buf, z_buf, a_buf, b_buf, g_buf, out_buf,
    spread, rows, w_t, g_t, full_t, bc_buf, bc_f32, b_t, sc_buf,
    f_buf, r_buf, o_buf, ent, d_send, d_buf, e_decay,
    x_sem, z_sem, out_sem, bc_sem, hx_sem, hb_sem, d_sem, f_sem, e_sem,
):
    n_ctx, n_head, tokens, channels = sizes
    chunks, tiles = tokens // CHUNK, channels // WIDE
    heads = channels // HEAD_DIM
    share = tokens // n_head
    c, h = lax.axis_index("ctx"), lax.axis_index("head")
    following, preceding = lax.rem(c + 1, n_ctx), lax.rem(c + n_ctx - 1, n_ctx)
    last_head = n_head - 1

    barrier = pltpu.get_barrier_semaphore()

    @pl.loop(1, n_head)
    def _(d):
        pl.semaphore_signal(barrier, inc=1, device_id=(c, lax.rem(h + d, n_head)), device_id_type=MESH)

    @pl.when(h != last_head)
    def _():
        pl.semaphore_signal(barrier, inc=1, device_id=(preceding, last_head), device_id_type=MESH)

    @pl.loop(1, n_ctx)
    def _(d):
        pl.semaphore_signal(barrier, inc=1, device_id=(lax.rem(c + d, n_ctx), h), device_id_type=MESH)

    def x_copy(q):
        part = pl.ds(q * CHUNK, CHUNK)
        return pltpu.make_async_copy(
            x_hbm.at[part], x_buf.at[pl.ds(HALO + q * CHUNK, CHUNK)], x_sem.at[q]
        )

    for q in range(chunks):
        x_copy(q).start()
    z_copy = pltpu.make_async_copy(z_hbm, z_buf, z_sem)
    z_copy.start()

    d_send[...] = jnp.zeros_like(d_send)
    sums = lax.dot_general(
        jnp.ones((8, tokens), F32), decay_ref[...], (((1,), (1,)), ((), ())),
        precision=HIGHEST, preferred_element_type=F32,
    )
    d_send[:, 0:heads] = sums[0:1]
    d_buf[c] = d_send[...]

    pl.semaphore_wait(barrier, n_ctx - 1 + n_head - 1 + jnp.where(h == last_head, n_head - 1, 0))

    def columns(t):
        return pl.ds(pl.multiple_of(t * STATE, STATE), STATE)

    mine = bc_buf.at[pl.ds(HALO + h * share, share)]

    @pl.loop(1, n_head)
    def _(d):
        t = lax.rem(h + d, n_head)
        pltpu.make_async_remote_copy(
            src_ref=bc_hbm.at[:, :, columns(t)], dst_ref=mine, send_sem=bc_sem.at[0], recv_sem=bc_sem.at[1],
            device_id=(c, t), device_id_type=MESH,
        ).start()

    own_bc = pltpu.make_async_copy(bc_hbm.at[:, :, columns(h)], mine, bc_sem.at[2])
    own_bc.start()

    @pl.when(h == last_head)
    def _():
        @pl.loop(0, n_head)
        def _(t):
            pltpu.make_async_remote_copy(
                src_ref=bc_hbm.at[pl.ds(share - HALO, HALO), :, columns(t)], dst_ref=bc_buf.at[pl.ds(0, HALO)],
                send_sem=hb_sem.at[0], recv_sem=hb_sem.at[1], device_id=(following, t), device_id_type=MESH,
            ).start()

    halo_x = pltpu.make_async_remote_copy(
        src_ref=x_hbm.at[pl.ds(tokens - HALO, HALO)], dst_ref=x_buf.at[pl.ds(0, HALO)],
        send_sem=hx_sem.at[0], recv_sem=hx_sem.at[1], device_id=(following, h), device_id_type=MESH,
    )
    halo_x.start()

    @pl.loop(1, n_ctx)
    def _(d):
        pltpu.make_async_remote_copy(
            src_ref=d_send, dst_ref=d_buf.at[c], send_sem=d_sem.at[0], recv_sem=d_sem.at[1],
            device_id=(lax.rem(c + d, n_ctx), h), device_id_type=MESH,
        ).start()

    head_of = lax.broadcasted_iota(jnp.int32, (2 * heads, channels), 1) // HEAD_DIM
    row_of = lax.rem(lax.broadcasted_iota(jnp.int32, (2 * heads, channels), 0), heads)
    spread[...] = (head_of == row_of).astype(F32).astype(BF16)

    upto = (
        lax.broadcasted_iota(jnp.int32, (CHUNK, CHUNK), 0) <= lax.broadcasted_iota(jnp.int32, (CHUNK, CHUNK), 1)
    ).astype(F32)
    before = jnp.zeros((heads, 1), F32)
    to_middle, to_end = [], []
    for q in range(chunks):
        part = slice(q * CHUNK, (q + 1) * CHUNK)
        cum = jnp.dot(decay_ref[:, part], upto, precision=HIGHEST, preferred_element_type=F32)
        middle, last = cum[:, CHUNK // 2 - 1 : CHUNK // 2], cum[:, CHUNK - 1 : CHUNK]
        w_t[q] = split(jnp.exp(middle - cum) * dt_ref[:, part])
        g_t[q] = split(jnp.exp(cum - middle))
        full_t[q] = split(jnp.exp(before + cum))
        to_middle.append(jnp.exp(middle))
        to_end.append(jnp.exp(last - middle))
        before = before + last
    lane = lax.broadcasted_iota(jnp.int32, (heads, 128), 1)
    packed = jnp.zeros((heads, 128), F32)
    for i, value in enumerate(to_middle + to_end):
        packed = jnp.where(lane == i, value, packed)
    eye = lax.broadcasted_iota(jnp.int32, (heads, heads), 0) == lax.broadcasted_iota(jnp.int32, (heads, heads), 1)
    skip_column = jnp.sum(jnp.where(eye, skip_ref[...], 0.0), axis=1, keepdims=True)
    packed = split(jnp.where(lane == 2 * chunks, skip_column, packed))
    for j in range(tiles):
        wide = slice(j * WIDE, (j + 1) * WIDE)
        rows[:, wide] = across(packed, spread[:, wide])[0 : rows.shape[0]]

    halo_x.wait_recv()

    @pl.when(c == 0)
    def _():
        x_buf[0:HALO] = jnp.zeros((HALO, channels), BF16)

    for q in range(chunks):
        x_copy(q).wait()

        @pl.loop(0, tiles)
        def _(j):
            wide = pl.ds(pl.multiple_of(j * WIDE, WIDE), WIDE)
            part = slice(q * CHUNK, (q + 1) * CHUNK)
            seen = x_buf[q * CHUNK : q * CHUNK + CHUNK + HALO, wide].astype(F32)
            half = 0.5 * xb_ref[:, wide]
            for tap in range(4):
                first = HALO - 3 + tap
                half = half + (0.5 * xk_ref[tap : tap + 1, wide]) * seen[first : first + CHUNK]
            xc = swish_of_twice(half).astype(BF16)
            xc_buf[part, wide] = xc
            xs_buf[q, 0:CHUNK, wide] = (xc.astype(F32) * across(w_t[q], spread[:, wide])).astype(BF16)

    others = bc_buf.at[pl.ds(0, tokens - share)]
    pltpu.make_async_copy(others, others, bc_sem.at[1]).wait()
    own_bc.wait()
    pltpu.make_async_copy(bc_buf.at[pl.ds(0, HALO)], bc_buf.at[pl.ds(0, HALO)], hb_sem.at[1]).wait()
    flat = bc_buf.reshape(2 * (tokens + HALO), STATE)
    bc_f32[0 : 2 * HALO] = jnp.where(c == 0, 0.0, flat[0 : 2 * HALO].astype(F32))
    causal = lax.broadcasted_iota(jnp.int32, (CHUNK, CHUNK), 0) >= lax.broadcasted_iota(jnp.int32, (CHUNK, CHUNK), 1)
    for q in range(chunks):
        first = 2 * (HALO + q * CHUNK)
        bc_f32[first : first + 2 * CHUNK] = flat[first : first + 2 * CHUNK].astype(F32)
        done = []
        for which in range(2):
            half = 0.5 * bcb_ref[which : which + 1]
            for tap in range(4):
                start = 2 * (HALO + q * CHUNK - 3 + tap) + which
                half = half + (0.5 * bck_ref[tap, which : which + 1]) * bc_f32[pl.ds(start, CHUNK, stride=2), :]
            done.append(swish_of_twice(half))
        b_t[q] = done[0].T.astype(BF16)
        b_part, c_part = done[0].astype(BF16), done[1].astype(BF16)
        scores = lax.dot_general(c_part, b_part, (((1,), (1,)), ((), ())), preferred_element_type=F32)
        sc_buf[q, :, 0:CHUNK] = jnp.where(causal, scores, 0.0).astype(BF16)
        sc_buf[q, :, CHUNK : CHUNK + STATE] = c_part

    def to_owner(k):
        return pltpu.make_async_remote_copy(
            src_ref=f_buf.at[k], dst_ref=r_buf.at[c], send_sem=f_sem.at[0], recv_sem=f_sem.at[1],
            device_id=(k, h), device_id_type=MESH,
        )

    per_tile = n_ctx // tiles
    deep = STATE * 128 // (STATE * channels // n_ctx)
    height = STATE // deep

    @pl.loop(0, tiles)
    def _(i):
        j = lax.rem(i + c // per_tile, tiles)
        wide = pl.ds(pl.multiple_of(j * WIDE, WIDE), WIDE)
        state = jnp.zeros((STATE, WIDE), F32)
        for q in range(chunks):
            scaled = state * rows[q : q + 1, wide]
            xs_buf[q, CHUNK : CHUNK + STATE, wide] = scaled.astype(BF16)
            fresh = dot(b_t[q], xs_buf[q, 0:CHUNK, wide])
            state = (scaled + fresh) * rows[chunks + q : chunks + q + 1, wide]
        for a in range(WIDE // 128):
            for b in range(deep):
                f_buf[j * per_tile + a * deep + b] = state[
                    b * height : (b + 1) * height, a * 128 : (a + 1) * 128
                ].astype(BF16)
        for s in range(per_tile):
            k = j * per_tile + s

            @pl.when(k != c)
            def _():
                to_owner(k).start()

    r_buf[c] = f_buf[c]
    z_copy.wait()

    def gate(first, end):
        @pl.loop(first * tiles, end * tiles)
        def _(i):
            q, j = i // tiles, lax.rem(i, tiles)
            wide = pl.ds(pl.multiple_of(j * WIDE, WIDE), WIDE)
            part = pl.ds(pl.multiple_of(q * CHUNK, CHUNK), CHUNK)
            y = dot(sc_buf[q], xs_buf[q, :, wide]) * across(g_t[q], spread[:, wide])
            y = y + rows[2 * chunks : 2 * chunks + 1, wide] * xc_buf[part, wide].astype(F32)
            swish = swish_of_twice(0.5 * z_buf[part, wide].astype(F32))
            a_buf[part, wide] = y * swish
            b_buf[part, wide] = across(full_t[q], spread[:, wide]) * swish

    gate(0, chunks)

    pltpu.make_async_copy(d_buf.at[pl.ds(0, n_ctx - 1)], d_buf.at[pl.ds(0, n_ctx - 1)], d_sem.at[1]).wait()
    pair = c // deep
    pick = (
        lax.broadcasted_iota(jnp.int32, (128, 128), 0)
        == 2 * pair + lax.broadcasted_iota(jnp.int32, (128, 128), 1) // HEAD_DIM
    ).astype(F32)
    totals = d_buf[...].reshape(n_ctx, 128)
    e_decay[...] = jnp.exp(jnp.dot(totals, pick, precision=HIGHEST, preferred_element_type=F32))
    pltpu.make_async_copy(r_buf.at[pl.ds(0, n_ctx - 1)], r_buf.at[pl.ds(0, n_ctx - 1)], f_sem.at[1]).wait()

    def advance(i, state):
        o_buf[i] = state.astype(BF16)
        return state * e_decay[pl.ds(i, 1), :] + r_buf[i].astype(F32)

    lax.fori_loop(0, n_ctx, advance, jnp.zeros((height, 128), F32))

    place = (
        pl.ds(pl.multiple_of(lax.rem(c, deep) * height, height), height),
        pl.ds(pl.multiple_of(pair * 128, 128), 128),
    )

    @pl.loop(1, n_ctx)
    def _(d):
        t = lax.rem(c + d, n_ctx)
        pltpu.make_async_remote_copy(
            src_ref=o_buf.at[t], dst_ref=ent.at[place], send_sem=e_sem.at[0], recv_sem=e_sem.at[1],
            device_id=(t, h), device_id_type=MESH,
        ).start()

    ent[place] = o_buf[c]
    pltpu.make_async_copy(o_buf.at[pl.ds(0, n_ctx - 1)], o_buf.at[pl.ds(0, n_ctx - 1)], e_sem.at[1]).wait()

    def out_copy(q):
        part = pl.ds(q * CHUNK, CHUNK)
        return pltpu.make_async_copy(out_buf.at[part], out_hbm.at[part], out_sem.at[q])

    for q in range(chunks):
        part = slice(q * CHUNK, (q + 1) * CHUNK)
        square = jnp.zeros((CHUNK, WIDE), F32)
        for j in range(tiles):
            wide = slice(j * WIDE, (j + 1) * WIDE)
            gated = a_buf[part, wide] + b_buf[part, wide] * dot(sc_buf[q, :, CHUNK : CHUNK + STATE], ent[:, wide])
            g_buf[:, wide] = gated
            square = square + gated * gated
        scale = lax.rsqrt(jnp.sum(square, axis=1, keepdims=True) * (1.0 / channels) + 1e-5)
        for j in range(tiles):
            wide = slice(j * WIDE, (j + 1) * WIDE)
            out_buf[part, wide] = (g_buf[:, wide] * scale * gain_ref[:, wide]).astype(BF16)
        out_copy(q).start()

    pltpu.make_async_copy(others, others, bc_sem.at[0]).wait()

    @pl.when(h == last_head)
    def _():
        sent = bc_buf.at[pl.ds(0, n_head * HALO)]
        pltpu.make_async_copy(sent, sent, hb_sem.at[0]).wait()

    halo_x.wait_send()
    for buffer, sem in ((d_buf, d_sem), (f_buf, f_sem), (o_buf, e_sem)):
        sent = buffer.at[pl.ds(0, n_ctx - 1)]
        pltpu.make_async_copy(sent, sent, sem.at[0]).wait()
    for q in range(chunks):
        out_copy(q).wait()


def per_device(
    n_ctx, n_head, x_in, bc_in, z_in, dt, log_decay, x_kernel, bc_kernel, x_bias, bc_bias, skip, norm_gain
):
    tokens, channels = x_in.shape
    heads = channels // HEAD_DIM
    chunks = tokens // CHUNK
    height = STATE * channels // n_ctx // 128
    anywhere, vmem = pl.BlockSpec(memory_space=pl.ANY), pl.BlockSpec(memory_space=pltpu.VMEM)
    dma = pltpu.SemaphoreType.DMA
    return pl.pallas_call(
        functools.partial(kernel, (n_ctx, n_head, tokens, channels)),
        out_shape=jax.ShapeDtypeStruct((tokens, channels), BF16),
        in_specs=[anywhere] * 3 + [vmem] * 8,
        out_specs=anywhere,
        scratch_shapes=[
            pltpu.VMEM((tokens + HALO, channels), BF16),
            pltpu.VMEM((tokens, channels), BF16),
            pltpu.VMEM((chunks, CHUNK + STATE, channels), BF16),
            pltpu.VMEM((tokens, channels), BF16),
            pltpu.VMEM((tokens, channels), F32),
            pltpu.VMEM((tokens, channels), F32),
            pltpu.VMEM((CHUNK, channels), F32),
            pltpu.VMEM((tokens, channels), BF16),
            pltpu.VMEM((2 * heads, channels), BF16),
            pltpu.VMEM((24, channels), F32),
            pltpu.VMEM((chunks, 2 * heads, CHUNK), BF16),
            pltpu.VMEM((chunks, 2 * heads, CHUNK), BF16),
            pltpu.VMEM((chunks, 2 * heads, CHUNK), BF16),
            pltpu.VMEM((tokens + HALO, 2, STATE), BF16),
            pltpu.VMEM((2 * (tokens + HALO), STATE), F32),
            pltpu.VMEM((chunks, STATE, CHUNK), BF16),
            pltpu.VMEM((chunks, CHUNK, CHUNK + STATE), BF16),
            pltpu.VMEM((n_ctx, height, 128), BF16),
            pltpu.VMEM((n_ctx, height, 128), BF16),
            pltpu.VMEM((n_ctx, height, 128), BF16),
            pltpu.VMEM((STATE, channels), BF16),
            pltpu.VMEM((1, 128), F32),
            pltpu.VMEM((n_ctx, 1, 128), F32),
            pltpu.VMEM((n_ctx, 128), F32),
            dma((chunks,)), dma, dma((chunks,)), dma((3,)), dma((2,)), dma((2,)), dma((2,)), dma((2,)), dma((2,)),
        ],
        compiler_params=pltpu.CompilerParams(
            collective_id=0, has_side_effects=True, vmem_limit_bytes=60 * 1024 * 1024
        ),
        cost_estimate=pl.CostEstimate(flops=2_500_000_000, bytes_accessed=14_000_000, transcendentals=5_000_000),
    )(
        x_in, bc_in, z_in, dt.T, log_decay.T, x_kernel, bc_kernel, x_bias[None], bc_bias, skip[None], norm_gain[None]
    )


def solution(mesh):
    placed = (
        P("ctx", "head"),
        P(("ctx", "head"), None, None),
        P("ctx", "head"),
        P("ctx", "head"),
        P("ctx", "head"),
        P(None, "head"),
        P(None, None, "head"),
        P("head"),
        P(None, "head"),
        P("head"),
        P("head"),
    )
    return jax.shard_map(
        functools.partial(per_device, mesh.shape["ctx"], mesh.shape["head"]),
        mesh=mesh, in_specs=placed, out_specs=P("ctx", "head"), check_vma=False,
    )
```

time: 385 us -> 74 us (0.19)
  the two profiles are of different devices: /device:TPU:230 before, /device:TPU:24 now
where the time goes in v1:
time: 74 us; the launch traced here: 73.9 us
  Pallas kernels  69.1 us (93%)
  local copies, waits for them, and re-layouts  4.79 us (6%)
    pallas_call x1, Pallas kernels, per_device(): pl.pallas_call(functools.partial(kernel, (n_ctx, n_head, tokens, channels...  69.1 us
    unnamed x1, local copies, waits for them, and re-layouts  4.79 us

profile of v1, /device:TPU:24, one launch (start us, length us, event | category | flops | bytes accessed | tf_op | source)
XLA Modules:
  0.0 73.9 jit_solution(7128959664987024891)
XLA Ops:
  0.0 69.1 %shard_map.109 = bf16[1024,2048]{1,0:T(8,128)(2,1)} custom-call(bf16[1024,2048]{1,0:T(8,128)(2,1)} %x_hbm.1, bf16[128,2,1024]{2,1,0:T(2,128)(2,1)} %bc_hbm.1, bf16[1024,2048]{1,0:T(8,128)(2,1)} %z_hbm.1, f32[32,1024]{1,0:T(8,128)} %bitcast.5, f32[32,1024]{1,0:T(8,128)} %bitcast.6, f32[4,2048]{1,0:T(4,128)} %xk_ref.1, f32[4,2,128]{2,1,0:T(2,128)} %bck_ref.1, ...), custom_call_target="tpu_custom_call" | custom-call | flops 2500000000 | bytes 14000000 | tf_op jit(solution)/shard_map/pallas_call | solution.py:326
  69.1 4.8 %copy.13 = bf16[1024,2048]{1,0:T(8,128)(2,1)} copy(bf16[1024,2048]{1,0:T(8,128)(2,1)} %shard_map.109) | data formatting | bytes 8388608

commit v2 on v1

--- a/solution.py
+++ b/solution.py
@@ -23,6 +23,11 @@
     return jnp.concatenate([high, low], axis=0)
 
 
+def split_columns(value):
+    high = value.astype(BF16).astype(F32)
+    return jnp.concatenate([high, value - high], axis=0).T.astype(BF16)
+
+
 def across(left, right):
     return lax.dot_general(left, right, (((0,), (0,)), ((), ())), preferred_element_type=F32)
 
@@ -37,12 +42,12 @@
 
 def kernel(
     sizes,
-    x_hbm, bc_hbm, z_hbm, dt_ref, decay_ref, xk_ref, bck_ref, xb_ref, bcb_ref, skip_ref, gain_ref,
-    out_hbm,
-    x_buf, xc_buf, xs_buf, z_buf, a_buf, b_buf, g_buf, out_buf,
-    spread, rows, w_t, g_t, full_t, bc_buf, bc_f32, b_t, sc_buf,
-    f_buf, r_buf, o_buf, ent, d_send, d_buf, e_decay,
-    x_sem, z_sem, out_sem, bc_sem, hx_sem, hb_sem, d_sem, f_sem, e_sem,
+    x_hbm, bc_hbm, z_hbm, dt_ref, decay_ref, xk_ref, bck_ref, xb_ref, bcb_ref, skip_ref,
+    a_buf, b_buf, c_buf, ent,
+    x_buf, xc_buf, xs_buf, z_buf,
+    spread, rows, w_t, g_t, full_t, shift, bc_buf, bc_f32, b_t, sc_buf,
+    f_buf, r_buf, o_buf, d_send, d_buf, e_decay,
+    x_sem, z_sem, bc_sem, hx_sem, hb_sem, d_sem, f_sem, e_sem,
 ):
     n_ctx, n_head, tokens, channels = sizes
     chunks, tiles = tokens // CHUNK, channels // WIDE
@@ -138,9 +143,9 @@
         part = slice(q * CHUNK, (q + 1) * CHUNK)
         cum = jnp.dot(decay_ref[:, part], upto, precision=HIGHEST, preferred_element_type=F32)
         middle, last = cum[:, CHUNK // 2 - 1 : CHUNK // 2], cum[:, CHUNK - 1 : CHUNK]
-        w_t[q] = split(jnp.exp(middle - cum) * dt_ref[:, part])
-        g_t[q] = split(jnp.exp(cum - middle))
-        full_t[q] = split(jnp.exp(before + cum))
+        w_t[q] = split_columns(jnp.exp(middle - cum) * dt_ref[:, part])
+        g_t[q] = split_columns(jnp.exp(cum - middle))
+        full_t[q] = split_columns(jnp.exp(before + cum))
         to_middle.append(jnp.exp(middle))
         to_end.append(jnp.exp(last - middle))
         before = before + last
@@ -155,27 +160,31 @@
         wide = slice(j * WIDE, (j + 1) * WIDE)
         rows[:, wide] = across(packed, spread[:, wide])[0 : rows.shape[0]]
 
+    row = lax.broadcasted_iota(jnp.int32, shift.shape, 0)
+    column = lax.broadcasted_iota(jnp.int32, shift.shape, 1)
+    shift[...] = (column == lax.rem(row, CHUNK) + row // CHUNK + HALO - 3).astype(F32).astype(BF16)
+
     halo_x.wait_recv()
 
     @pl.when(c == 0)
     def _():
         x_buf[0:HALO] = jnp.zeros((HALO, channels), BF16)
 
-    for q in range(chunks):
+    @pl.loop(0, chunks)
+    def _(q):
         x_copy(q).wait()
-
-        @pl.loop(0, tiles)
-        def _(j):
-            wide = pl.ds(pl.multiple_of(j * WIDE, WIDE), WIDE)
-            part = slice(q * CHUNK, (q + 1) * CHUNK)
-            seen = x_buf[q * CHUNK : q * CHUNK + CHUNK + HALO, wide].astype(F32)
-            half = 0.5 * xb_ref[:, wide]
-            for tap in range(4):
-                first = HALO - 3 + tap
-                half = half + (0.5 * xk_ref[tap : tap + 1, wide]) * seen[first : first + CHUNK]
-            xc = swish_of_twice(half).astype(BF16)
-            xc_buf[part, wide] = xc
-            xs_buf[q, 0:CHUNK, wide] = (xc.astype(F32) * across(w_t[q], spread[:, wide])).astype(BF16)
+        part = pl.ds(pl.multiple_of(q * CHUNK, CHUNK), CHUNK)
+        around = pl.ds(pl.multiple_of(q * CHUNK, CHUNK), CHUNK + HALO)
+        for j in range(tiles):
+            wide = slice(j * WIDE, (j + 1) * WIDE)
+            seen = x_buf[around, wide]
+            moved = dot(shift[...], seen)
+            half = 0.5 * xb_ref[:, wide] + (0.5 * xk_ref[3:4, wide]) * seen[HALO:].astype(F32)
+            for tap in range(3):
+                half = half + (0.5 * xk_ref[tap : tap + 1, wide]) * moved[tap * CHUNK : (tap + 1) * CHUNK]
+            xc = swish_of_twice(half)
+            xc_buf[part, wide] = xc.astype(BF16)
+            xs_buf[q, 0:CHUNK, wide] = (xc * dot(w_t[q], spread[:, wide])).astype(BF16)
 
     others = bc_buf.at[pl.ds(0, tokens - share)]
     pltpu.make_async_copy(others, others, bc_sem.at[1]).wait()
@@ -199,6 +208,7 @@
         scores = lax.dot_general(c_part, b_part, (((1,), (1,)), ((), ())), preferred_element_type=F32)
         sc_buf[q, :, 0:CHUNK] = jnp.where(causal, scores, 0.0).astype(BF16)
         sc_buf[q, :, CHUNK : CHUNK + STATE] = c_part
+        c_buf[q * CHUNK : (q + 1) * CHUNK] = c_part
 
     def to_owner(k):
         return pltpu.make_async_remote_copy(
@@ -236,18 +246,18 @@
     z_copy.wait()
 
     def gate(first, end):
-        @pl.loop(first * tiles, end * tiles)
-        def _(i):
-            q, j = i // tiles, lax.rem(i, tiles)
-            wide = pl.ds(pl.multiple_of(j * WIDE, WIDE), WIDE)
+        @pl.loop(first, end)
+        def _(q):
             part = pl.ds(pl.multiple_of(q * CHUNK, CHUNK), CHUNK)
-            y = dot(sc_buf[q], xs_buf[q, :, wide]) * across(g_t[q], spread[:, wide])
-            y = y + rows[2 * chunks : 2 * chunks + 1, wide] * xc_buf[part, wide].astype(F32)
-            swish = swish_of_twice(0.5 * z_buf[part, wide].astype(F32))
-            a_buf[part, wide] = y * swish
-            b_buf[part, wide] = across(full_t[q], spread[:, wide]) * swish
-
-    gate(0, chunks)
+            for j in range(tiles):
+                wide = slice(j * WIDE, (j + 1) * WIDE)
+                y = dot(sc_buf[q], xs_buf[q, :, wide]) * dot(g_t[q], spread[:, wide])
+                y = y + rows[2 * chunks : 2 * chunks + 1, wide] * xc_buf[part, wide].astype(F32)
+                swish = swish_of_twice(0.5 * z_buf[part, wide].astype(F32))
+                a_buf[part, wide] = y * swish
+                b_buf[part, wide] = dot(full_t[q], spread[:, wide]) * swish
+
+    gate(0, chunks // 2)
 
     pltpu.make_async_copy(d_buf.at[pl.ds(0, n_ctx - 1)], d_buf.at[pl.ds(0, n_ctx - 1)], d_sem.at[1]).wait()
     pair = c // deep
@@ -279,18 +289,37 @@
         ).start()
 
     ent[place] = o_buf[c]
+    gate(chunks // 2, chunks)
     pltpu.make_async_copy(o_buf.at[pl.ds(0, n_ctx - 1)], o_buf.at[pl.ds(0, n_ctx - 1)], e_sem.at[1]).wait()
 
+    pltpu.make_async_copy(others, others, bc_sem.at[0]).wait()
+
+    @pl.when(h == last_head)
+    def _():
+        sent = bc_buf.at[pl.ds(0, n_head * HALO)]
+        pltpu.make_async_copy(sent, sent, hb_sem.at[0]).wait()
+
+    halo_x.wait_send()
+    for buffer, sem in ((d_buf, d_sem), (f_buf, f_sem), (o_buf, e_sem)):
+        sent = buffer.at[pl.ds(0, n_ctx - 1)]
+        pltpu.make_async_copy(sent, sent, sem.at[0]).wait()
+
+
+def finish(a_ref, b_ref, c_ref, ent_ref, gain_ref, out_hbm, g_buf, out_buf, out_sem):
+    tokens, channels = a_ref.shape
+    chunks, tiles = tokens // CHUNK, channels // WIDE
+
     def out_copy(q):
-        part = pl.ds(q * CHUNK, CHUNK)
+        part = pl.ds(pl.multiple_of(q * CHUNK, CHUNK), CHUNK)
         return pltpu.make_async_copy(out_buf.at[part], out_hbm.at[part], out_sem.at[q])
 
-    for q in range(chunks):
-        part = slice(q * CHUNK, (q + 1) * CHUNK)
+    @pl.loop(0, chunks)
+    def _(q):
+        part = pl.ds(pl.multiple_of(q * CHUNK, CHUNK), CHUNK)
         square = jnp.zeros((CHUNK, WIDE), F32)
         for j in range(tiles):
             wide = slice(j * WIDE, (j + 1) * WIDE)
-            gated = a_buf[part, wide] + b_buf[part, wide] * dot(sc_buf[q, :, CHUNK : CHUNK + STATE], ent[:, wide])
+            gated = a_ref[part, wide] + b_ref[part, wide] * dot(c_ref[part], ent_ref[:, wide])
             g_buf[:, wide] = gated
             square = square + gated * gated
         scale = lax.rsqrt(jnp.sum(square, axis=1, keepdims=True) * (1.0 / channels) + 1e-5)
@@ -299,18 +328,8 @@
             out_buf[part, wide] = (g_buf[:, wide] * scale * gain_ref[:, wide]).astype(BF16)
         out_copy(q).start()
 
-    pltpu.make_async_copy(others, others, bc_sem.at[0]).wait()
-
-    @pl.when(h == last_head)
-    def _():
-        sent = bc_buf.at[pl.ds(0, n_head * HALO)]
-        pltpu.make_async_copy(sent, sent, hb_sem.at[0]).wait()
-
-    halo_x.wait_send()
-    for buffer, sem in ((d_buf, d_sem), (f_buf, f_sem), (o_buf, e_sem)):
-        sent = buffer.at[pl.ds(0, n_ctx - 1)]
-        pltpu.make_async_copy(sent, sent, sem.at[0]).wait()
-    for q in range(chunks):
+    @pl.loop(0, chunks)
+    def _(q):
         out_copy(q).wait()
 
 
@@ -323,25 +342,27 @@
     height = STATE * channels // n_ctx // 128
     anywhere, vmem = pl.BlockSpec(memory_space=pl.ANY), pl.BlockSpec(memory_space=pltpu.VMEM)
     dma = pltpu.SemaphoreType.DMA
-    return pl.pallas_call(
+    a, b, c_part, ent = pl.pallas_call(
         functools.partial(kernel, (n_ctx, n_head, tokens, channels)),
-        out_shape=jax.ShapeDtypeStruct((tokens, channels), BF16),
-        in_specs=[anywhere] * 3 + [vmem] * 8,
-        out_specs=anywhere,
+        out_shape=[
+            pltpu.VMEM((tokens, channels), F32),
+            pltpu.VMEM((tokens, channels), F32),
+            pltpu.VMEM((tokens, STATE), BF16),
+            pltpu.VMEM((STATE, channels), BF16),
+        ],
+        in_specs=[anywhere] * 3 + [vmem] * 7,
+        out_specs=[vmem] * 4,
         scratch_shapes=[
             pltpu.VMEM((tokens + HALO, channels), BF16),
             pltpu.VMEM((tokens, channels), BF16),
             pltpu.VMEM((chunks, CHUNK + STATE, channels), BF16),
             pltpu.VMEM((tokens, channels), BF16),
-            pltpu.VMEM((tokens, channels), F32),
-            pltpu.VMEM((tokens, channels), F32),
-            pltpu.VMEM((CHUNK, channels), F32),
-            pltpu.VMEM((tokens, channels), BF16),
             pltpu.VMEM((2 * heads, channels), BF16),
             pltpu.VMEM((24, channels), F32),
-            pltpu.VMEM((chunks, 2 * heads, CHUNK), BF16),
-            pltpu.VMEM((chunks, 2 * heads, CHUNK), BF16),
-            pltpu.VMEM((chunks, 2 * heads, CHUNK), BF16),
+            pltpu.VMEM((chunks, CHUNK, 2 * heads), BF16),
+            pltpu.VMEM((chunks, CHUNK, 2 * heads), BF16),
+            pltpu.VMEM((chunks, CHUNK, 2 * heads), BF16),
+            pltpu.VMEM((3 * CHUNK, CHUNK + HALO), BF16),
             pltpu.VMEM((tokens + HALO, 2, STATE), BF16),
             pltpu.VMEM((2 * (tokens + HALO), STATE), F32),
             pltpu.VMEM((chunks, STATE, CHUNK), BF16),
@@ -349,19 +370,29 @@
             pltpu.VMEM((n_ctx, height, 128), BF16),
             pltpu.VMEM((n_ctx, height, 128), BF16),
             pltpu.VMEM((n_ctx, height, 128), BF16),
-            pltpu.VMEM((STATE, channels), BF16),
             pltpu.VMEM((1, 128), F32),
             pltpu.VMEM((n_ctx, 1, 128), F32),
             pltpu.VMEM((n_ctx, 128), F32),
-            dma((chunks,)), dma, dma((chunks,)), dma((3,)), dma((2,)), dma((2,)), dma((2,)), dma((2,)), dma((2,)),
+            dma((chunks,)), dma, dma((3,)), dma((2,)), dma((2,)), dma((2,)), dma((2,)), dma((2,)),
         ],
         compiler_params=pltpu.CompilerParams(
-            collective_id=0, has_side_effects=True, vmem_limit_bytes=60 * 1024 * 1024
+            collective_id=0, has_side_effects=True, vmem_limit_bytes=45_900_000
         ),
-        cost_estimate=pl.CostEstimate(flops=2_500_000_000, bytes_accessed=14_000_000, transcendentals=5_000_000),
-    )(
-        x_in, bc_in, z_in, dt.T, log_decay.T, x_kernel, bc_kernel, x_bias[None], bc_bias, skip[None], norm_gain[None]
-    )
+        cost_estimate=pl.CostEstimate(flops=2_500_000_000, bytes_accessed=10_000_000, transcendentals=5_000_000),
+    )(x_in, bc_in, z_in, dt.T, log_decay.T, x_kernel, bc_kernel, x_bias[None], bc_bias, skip[None])
+    return pl.pallas_call(
+        finish,
+        out_shape=jax.ShapeDtypeStruct((tokens, channels), BF16),
+        in_specs=[vmem] * 5,
+        out_specs=anywhere,
+        scratch_shapes=[
+            pltpu.VMEM((CHUNK, channels), F32),
+            pltpu.VMEM((tokens, channels), BF16),
+            dma((chunks,)),
+        ],
+        compiler_params=pltpu.CompilerParams(vmem_limit_bytes=16 * 1024 * 1024),
+        cost_estimate=pl.CostEstimate(flops=600_000_000, bytes_accessed=4_000_000, transcendentals=1_000),
+    )(a, b, c_part, ent, norm_gain[None])
 
 
 def solution(mesh):

time: 74 us -> 55.4 us (0.75)
  the two profiles are of different devices: /device:TPU:24 before, /device:TPU:30 now
where the time goes in v2:
time: 55.4 us; the launch traced here: 55.3 us
  Pallas kernels  55.3 us (100%)
    pallas_call x1, Pallas kernels, per_device(): pl.pallas_call(functools.partial(kernel, (n_ctx, n_head, tokens, channels...  50.8 us
    pallas_call x1, Pallas kernels, per_device(): pl.pallas_call(finish, out_shape=jax.ShapeDtypeStruct((tokens, channels),...  4.46 us

profile of v2, /device:TPU:30, one launch (start us, length us, event | category | flops | bytes accessed | tf_op | source)
XLA Modules:
  0.0 55.3 jit_solution(11110517544001928575)
XLA Ops:
  0.0 0.0 copy-start
  0.0 50.8 %shard_map.109 = (f32[1024,2048]{1,0:T(8,128)S(1)}, f32[1024,2048]{1,0:T(8,128)S(1)}, bf16[1024,128]{1,0:T(8,128)(2,1)S(1)}, bf16[128,2048]{1,0:T(8,128)(2,1)S(1)}) custom-call(bf16[1024,2048]{1,0:T(8,128)(2,1)} %x_hbm.1, bf16[128,2,1024]{2,1,0:T(2,128)(2,1)} %bc_hbm.1, bf16[1024,2048]{1,0:T(8,128)(2,1)} %z_hbm.1, f32[32,1024]{1,0:T(8,128)} %bitcast.6, ...), custom_call_target="tpu_custom_call" | custom-call | flops 2500000000 | bytes 10000000 | tf_op jit(solution)/shard_map/pallas_call | solution.py:345
  50.8 0.0 copy-done
  50.8 4.5 %shard_map.110 = bf16[1024,2048]{1,0:T(8,128)(2,1)} custom-call(f32[1024,2048]{1,0:T(8,128)S(1)} %get-tuple-element.9.a_ref, f32[1024,2048]{1,0:T(8,128)S(1)} %get-tuple-element.10.b_ref, bf16[1024,128]{1,0:T(8,128)(2,1)S(1)} %get-tuple-element.11.c_ref, bf16[128,2048]{1,0:T(8,128)(2,1)S(1)} %get-tuple-element.12.ent_ref, f32[1,2048]{1,0:T(1,128)S(1)} %bitcast.5), custom_call_target="tpu_custom_call" | custom-call | flops 600000000 | bytes 4000000 | tf_op jit(solution)/shard_map/pallas_call | solution.py:383
Async XLA Ops:
  0.0 50.8 %copy-start = (f32[2048]{0:T(1024)S(1)}, f32[2048]{0:T(1024)}, u32[]{:S(2)}) copy-start(f32[2048]{0:T(1024)} %param.21) | copy-start | bytes 24580

commit v3 on v2

v3 whole, which is shorter than its diff:
```python
import functools

import jax
import jax.numpy as jnp
from jax import lax
from jax.experimental import pallas as pl
from jax.experimental.pallas import tpu as pltpu
from jax.sharding import PartitionSpec as P

MESH = pl.DeviceIdType.MESH
F32, BF16 = jnp.float32, jnp.bfloat16
HEAD_DIM = 64
STATE = 128
CHUNK = 128
HALO = 16
WIDE = 256
PARTS = 2
HIGHEST = lax.Precision.HIGHEST


def split(value):
    high = value.astype(BF16)
    low = (value - high.astype(F32)).astype(BF16)
    return jnp.concatenate([high, low], axis=0)


def split_columns(value):
    high = value.astype(BF16).astype(F32)
    return jnp.concatenate([high, value - high], axis=0).T.astype(BF16)


def across(left, right):
    return lax.dot_general(left, right, (((0,), (0,)), ((), ())), preferred_element_type=F32)


def dot(left, right):
    return jnp.dot(left, right, preferred_element_type=F32)


def swish_of_twice(half):
    return half + half * jnp.tanh(half)


def kernel(
    sizes,
    x_hbm, bc_hbm, z_hbm, dt_ref, decay_ref, xk_ref, bck_ref, xb_ref, bcb_ref, skip_ref,
    a_buf, b_buf, c_buf, ent,
    x_buf, xc_buf, xs_buf, z_buf,
    spread, rows, w_t, g_t, full_t, shift, bc_raw, bc_f32, bc_send, bc_buf, b_conv, b_t, sc_buf,
    f_buf, r_buf, o_buf, d_send, d_buf, e_decay,
    x_sem, z_sem, raw_sem, bc_sem, hx_sem, hb_sem, d_sem, f_sem, e_sem,
):
    n_ctx, n_head, tokens, channels = sizes
    chunks, tiles = tokens // CHUNK, channels // WIDE
    heads = channels // HEAD_DIM
    share = tokens // n_head
    c, h = lax.axis_index("ctx"), lax.axis_index("head")
    following, preceding = lax.rem(c + 1, n_ctx), lax.rem(c + n_ctx - 1, n_ctx)
    last_head = n_head - 1

    barrier = pltpu.get_barrier_semaphore()

    @pl.loop(1, n_head)
    def _(d):
        pl.semaphore_signal(barrier, inc=1, device_id=(c, lax.rem(h + d, n_head)), device_id_type=MESH)

    @pl.when(h != last_head)
    def _():
        pl.semaphore_signal(barrier, inc=1, device_id=(preceding, last_head), device_id_type=MESH)

    @pl.loop(1, n_ctx)
    def _(d):
        pl.semaphore_signal(barrier, inc=1, device_id=(lax.rem(c + d, n_ctx), h), device_id_type=MESH)

    def columns(t):
        return pl.ds(pl.multiple_of(t * STATE, STATE), STATE)

    def raw_copy(t):
        return pltpu.make_async_copy(
            bc_hbm.at[:, :, t * STATE : (t + 1) * STATE], bc_raw.at[pl.ds(t * share, share)], raw_sem.at[t]
        )

    def x_copy(q):
        part = pl.ds(q * CHUNK, CHUNK)
        return pltpu.make_async_copy(
            x_hbm.at[part], x_buf.at[pl.ds(HALO + q * CHUNK, CHUNK)], x_sem.at[q]
        )

    for t in range(n_head):
        raw_copy(t).start()
    for q in range(chunks):
        x_copy(q).start()
    z_copy = pltpu.make_async_copy(z_hbm, z_buf, z_sem)
    z_copy.start()

    d_send[...] = jnp.zeros_like(d_send)
    sums = lax.dot_general(
        jnp.ones((8, tokens), F32), decay_ref[...], (((1,), (1,)), ((), ())),
        precision=HIGHEST, preferred_element_type=F32,
    )
    d_send[:, 0:heads] = sums[0:1]
    d_buf[c] = d_send[...]

    flat = bc_raw.reshape(2 * tokens, STATE)
    for t in range(n_head):
        raw_copy(t).wait()
        bc_f32[...] = flat[2 * t * share : 2 * (t + 1) * share].astype(F32)
        for which in range(2):
            bc_send[which, t] = bc_f32[pl.ds(which, share, stride=2), :].astype(BF16)

    head_of = lax.broadcasted_iota(jnp.int32, (2 * heads, channels), 1) // HEAD_DIM
    row_of = lax.rem(lax.broadcasted_iota(jnp.int32, (2 * heads, channels), 0), heads)
    spread[...] = (head_of == row_of).astype(F32).astype(BF16)

    upto = (
        lax.broadcasted_iota(jnp.int32, (CHUNK, CHUNK), 0) <= lax.broadcasted_iota(jnp.int32, (CHUNK, CHUNK), 1)
    ).astype(F32)
    before = jnp.zeros((heads, 1), F32)
    to_middle, to_end = [], []
    for q in range(chunks):
        part = slice(q * CHUNK, (q + 1) * CHUNK)
        cum = jnp.dot(decay_ref[:, part], upto, precision=HIGHEST, preferred_element_type=F32)
        middle, last = cum[:, CHUNK // 2 - 1 : CHUNK // 2], cum[:, CHUNK - 1 : CHUNK]
        w_t[q] = split_columns(jnp.exp(middle - cum) * dt_ref[:, part])
        g_t[q] = split_columns(jnp.exp(cum - middle))
        full_t[q] = split_columns(jnp.exp(before + cum))
        to_middle.append(jnp.exp(middle))
        to_end.append(jnp.exp(last - middle))
        before = before + last
    lane = lax.broadcasted_iota(jnp.int32, (heads, 128), 1)
    packed = jnp.zeros((heads, 128), F32)
    for i, value in enumerate(to_middle + to_end):
        packed = jnp.where(lane == i, value, packed)
    eye = lax.broadcasted_iota(jnp.int32, (heads, heads), 0) == lax.broadcasted_iota(jnp.int32, (heads, heads), 1)
    skip_column = jnp.sum(jnp.where(eye, skip_ref[...], 0.0), axis=1, keepdims=True)
    packed = split(jnp.where(lane == 2 * chunks, skip_column, packed))
    for j in range(tiles):
        wide = slice(j * WIDE, (j + 1) * WIDE)
        rows[:, wide] = across(packed, spread[:, wide])[0 : rows.shape[0]]

    row = lax.broadcasted_iota(jnp.int32, shift.shape, 0)
    column = lax.broadcasted_iota(jnp.int32, shift.shape, 1)
    shift[...] = (column == lax.rem(row, CHUNK) + row // CHUNK + HALO - 3).astype(F32).astype(BF16)

    pl.semaphore_wait(barrier, n_ctx - 1 + n_head - 1 + jnp.where(h == last_head, n_head - 1, 0))

    mine = pl.ds(pl.multiple_of(HALO + h * share, HALO), share)
    halo_x = pltpu.make_async_remote_copy(
        src_ref=x_hbm.at[pl.ds(tokens - HALO, HALO)], dst_ref=x_buf.at[pl.ds(0, HALO)],
        send_sem=hx_sem.at[0], recv_sem=hx_sem.at[1], device_id=(following, h), device_id_type=MESH,
    )

    for which in range(2):
        @pl.loop(1, n_head)
        def _(d):
            t = lax.rem(h + d, n_head)
            pltpu.make_async_remote_copy(
                src_ref=bc_send.at[which, t], dst_ref=bc_buf.at[which, mine],
                send_sem=bc_sem.at[2 * which], recv_sem=bc_sem.at[2 * which + 1],
                device_id=(c, t), device_id_type=MESH,
            ).start()

        @pl.when(h == last_head)
        def _():
            @pl.loop(0, n_head)
            def _(t):
                pltpu.make_async_remote_copy(
                    src_ref=bc_send.at[which, t, pl.ds(share - HALO, HALO)], dst_ref=bc_buf.at[which, pl.ds(0, HALO)],
                    send_sem=hb_sem.at[2 * which], recv_sem=hb_sem.at[2 * which + 1],
                    device_id=(following, t), device_id_type=MESH,
                ).start()

        if which == 0:
            halo_x.start()
        bc_buf[which, mine] = bc_send[which, h]

    @pl.loop(1, n_ctx)
    def _(d):
        pltpu.make_async_remote_copy(
            src_ref=d_send, dst_ref=d_buf.at[c], send_sem=d_sem.at[0], recv_sem=d_sem.at[1],
            device_id=(lax.rem(c + d, n_ctx), h), device_id_type=MESH,
        ).start()

    x_copy(0).wait()

    @pl.loop(0, chunks)
    def _(i):
        q = lax.rem(i + 1, chunks)

        @pl.when(q != 0)
        def _():
            x_copy(q).wait()

        @pl.when(q == 0)
        def _():
            halo_x.wait_recv()

            @pl.when(c == 0)
            def _():
                x_buf[0:HALO] = jnp.zeros((HALO, channels), BF16)

        part = pl.ds(pl.multiple_of(q * CHUNK, CHUNK), CHUNK)
        around = pl.ds(pl.multiple_of(q * CHUNK, CHUNK), CHUNK + HALO)
        for j in range(tiles):
            wide = slice(j * WIDE, (j + 1) * WIDE)
            seen = x_buf[around, wide]
            moved = dot(shift[...], seen)
            half = 0.5 * xb_ref[:, wide] + (0.5 * xk_ref[3:4, wide]) * seen[HALO:].astype(F32)
            for tap in range(3):
                half = half + (0.5 * xk_ref[tap : tap + 1, wide]) * moved[tap * CHUNK : (tap + 1) * CHUNK]
            xc = swish_of_twice(half)
            xc_buf[part, wide] = xc.astype(BF16)
            xs_buf[q, 0:CHUNK, wide] = (xc * dot(w_t[q], spread[:, wide])).astype(BF16)

    def others(which):
        return bc_buf.at[which, pl.ds(0, tokens - share)]

    def arrived(which):
        pltpu.make_async_copy(others(which), others(which), bc_sem.at[2 * which + 1]).wait()
        rim = bc_buf.at[which, pl.ds(0, HALO)]
        pltpu.make_async_copy(rim, rim, hb_sem.at[2 * which + 1]).wait()

        @pl.when(c == 0)
        def _():
            bc_buf[which, 0:HALO] = jnp.zeros((HALO, STATE), BF16)

    def convolved(which, q):
        seen = bc_buf[which, q * CHUNK : q * CHUNK + CHUNK + HALO]
        moved = dot(shift[...], seen)
        half = 0.5 * bcb_ref[which : which + 1] + (0.5 * bck_ref[3, which : which + 1]) * seen[HALO:].astype(F32)
        for tap in range(3):
            half = half + (0.5 * bck_ref[tap, which : which + 1]) * moved[tap * CHUNK : (tap + 1) * CHUNK]
        return swish_of_twice(half)

    arrived(0)
    for q in range(chunks):
        b_part = convolved(0, q)
        b_conv[q * CHUNK : (q + 1) * CHUNK] = b_part.astype(BF16)
        b_t[q] = b_part.T.astype(BF16)

    deep = n_ctx * 128 * PARTS // channels
    height = STATE // deep
    part_tiles = tiles // PARTS
    per_tile = n_ctx // part_tiles

    def to_owner(p, k):
        return pltpu.make_async_remote_copy(
            src_ref=f_buf.at[p, k], dst_ref=r_buf.at[p, c], send_sem=f_sem.at[2 * p], recv_sem=f_sem.at[2 * p + 1],
            device_id=(k, h), device_id_type=MESH,
        )

    for p in range(PARTS):
        @pl.loop(0, part_tiles)
        def _(i):
            j = lax.rem(i + c // per_tile, part_tiles)
            wide = pl.ds(pl.multiple_of((p * part_tiles + j) * WIDE, WIDE), WIDE)
            state = jnp.zeros((STATE, WIDE), F32)
            for q in range(chunks):
                scaled = state * rows[q : q + 1, wide]
                xs_buf[q, CHUNK : CHUNK + STATE, wide] = scaled.astype(BF16)
                fresh = dot(b_t[q], xs_buf[q, 0:CHUNK, wide])
                state = (scaled + fresh) * rows[chunks + q : chunks + q + 1, wide]
            for a in range(WIDE // 128):
                for b in range(deep):
                    f_buf[p, j * per_tile + a * deep + b] = state[
                        b * height : (b + 1) * height, a * 128 : (a + 1) * 128
                    ].astype(BF16)

            @pl.loop(0, per_tile)
            def _(s):
                k = j * per_tile + s

                @pl.when(k != c)
                def _():
                    to_owner(p, k).start()

        r_buf[p, c] = f_buf[p, c]

    arrived(1)
    causal = lax.broadcasted_iota(jnp.int32, (CHUNK, CHUNK), 0) >= lax.broadcasted_iota(jnp.int32, (CHUNK, CHUNK), 1)
    for q in range(chunks):
        b_part, c_part = b_conv[q * CHUNK : (q + 1) * CHUNK], convolved(1, q).astype(BF16)
        scores = lax.dot_general(c_part, b_part, (((1,), (1,)), ((), ())), preferred_element_type=F32)
        sc_buf[q, :, 0:CHUNK] = jnp.where(causal, scores, 0.0).astype(BF16)
        sc_buf[q, :, CHUNK : CHUNK + STATE] = c_part
        c_buf[q * CHUNK : (q + 1) * CHUNK] = c_part
    z_copy.wait()

    def gate(first, end):
        @pl.loop(first, end)
        def _(q):
            part = pl.ds(pl.multiple_of(q * CHUNK, CHUNK), CHUNK)
            for j in range(tiles):
                wide = slice(j * WIDE, (j + 1) * WIDE)
                y = dot(sc_buf[q], xs_buf[q, :, wide]) * dot(g_t[q], spread[:, wide])
                y = y + rows[2 * chunks : 2 * chunks + 1, wide] * xc_buf[part, wide].astype(F32)
                swish = swish_of_twice(0.5 * z_buf[part, wide].astype(F32))
                a_buf[part, wide] = y * swish
                b_buf[part, wide] = dot(full_t[q], spread[:, wide]) * swish

    pltpu.make_async_copy(d_buf.at[pl.ds(0, n_ctx - 1)], d_buf.at[pl.ds(0, n_ctx - 1)], d_sem.at[1]).wait()
    totals = d_buf[...].reshape(n_ctx, 128)

    def pair(p):
        return p * (channels // 128 // PARTS) + c // deep

    for p in range(PARTS):
        pick = (
            lax.broadcasted_iota(jnp.int32, (128, 128), 0)
            == 2 * pair(p) + lax.broadcasted_iota(jnp.int32, (128, 128), 1) // HEAD_DIM
        ).astype(F32)
        e_decay[p] = jnp.exp(jnp.dot(totals, pick, precision=HIGHEST, preferred_element_type=F32))

    def scan(p):
        pltpu.make_async_copy(
            r_buf.at[p, pl.ds(0, n_ctx - 1)], r_buf.at[p, pl.ds(0, n_ctx - 1)], f_sem.at[2 * p + 1]
        ).wait()

        state = jnp.zeros((height, 128), F32)
        for i in range(n_ctx):
            o_buf[p, i] = state.astype(BF16)
            state = state * e_decay[p, i : i + 1, :] + r_buf[p, i].astype(F32)

        place = (
            pl.ds(pl.multiple_of(lax.rem(c, deep) * height, height), height),
            pl.ds(pl.multiple_of(pair(p) * 128, 128), 128),
        )

        @pl.loop(1, n_ctx)
        def _(d):
            t = lax.rem(c + d, n_ctx)
            pltpu.make_async_remote_copy(
                src_ref=o_buf.at[p, t], dst_ref=ent.at[place], send_sem=e_sem.at[2 * p], recv_sem=e_sem.at[2 * p + 1],
                device_id=(t, h), device_id_type=MESH,
            ).start()

        ent[place] = o_buf[p, c]

    def entered(p):
        pltpu.make_async_copy(
            o_buf.at[p, pl.ds(0, n_ctx - 1)], o_buf.at[p, pl.ds(0, n_ctx - 1)], e_sem.at[2 * p + 1]
        ).wait()

    gate(0, chunks // 2)
    scan(0)
    gate(chunks // 2, chunks - 1)
    scan(1)
    gate(chunks - 1, chunks)

    entered(0)

    @pl.loop(0, chunks)
    def _(q):
        part = pl.ds(pl.multiple_of(q * CHUNK, CHUNK), CHUNK)
        for j in range(part_tiles):
            wide = slice(j * WIDE, (j + 1) * WIDE)
            a_buf[part, wide] = a_buf[part, wide] + b_buf[part, wide] * dot(c_buf[part], ent[:, wide])

    for p in range(1, PARTS):
        entered(p)

    for which in range(2):
        pltpu.make_async_copy(others(which), others(which), bc_sem.at[2 * which]).wait()

    @pl.when(h == last_head)
    def _():
        for which in range(2):
            sent = bc_buf.at[which, pl.ds(0, n_head * HALO)]
            pltpu.make_async_copy(sent, sent, hb_sem.at[2 * which]).wait()

    halo_x.wait_send()
    sent = d_buf.at[pl.ds(0, n_ctx - 1)]
    pltpu.make_async_copy(sent, sent, d_sem.at[0]).wait()
    for buffer, sem in ((f_buf, f_sem), (o_buf, e_sem)):
        for p in range(PARTS):
            sent = buffer.at[p, pl.ds(0, n_ctx - 1)]
            pltpu.make_async_copy(sent, sent, sem.at[2 * p]).wait()


def finish(a_ref, b_ref, c_ref, ent_ref, gain_ref, out_hbm, g_buf, out_buf, out_sem):
    tokens, channels = a_ref.shape
    chunks, tiles = tokens // CHUNK, channels // WIDE

    def out_copy(q):
        part = pl.ds(pl.multiple_of(q * CHUNK, CHUNK), CHUNK)
        return pltpu.make_async_copy(out_buf.at[part], out_hbm.at[part], out_sem.at[q])

    @pl.loop(0, chunks)
    def _(q):
        part = pl.ds(pl.multiple_of(q * CHUNK, CHUNK), CHUNK)
        square = jnp.zeros((CHUNK, WIDE), F32)
        for j in range(tiles):
            wide = slice(j * WIDE, (j + 1) * WIDE)
            gated = a_ref[part, wide]
            if j >= tiles // PARTS:
                gated = gated + b_ref[part, wide] * dot(c_ref[part], ent_ref[:, wide])
                g_buf[:, wide] = gated
            square = square + gated * gated
        scale = lax.rsqrt(jnp.sum(square, axis=1, keepdims=True) * (1.0 / channels) + 1e-5)
        for j in range(tiles):
            wide = slice(j * WIDE, (j + 1) * WIDE)
            gated = a_ref[part, wide] if j < tiles // PARTS else g_buf[:, wide]
            out_buf[part, wide] = (gated * scale * gain_ref[:, wide]).astype(BF16)
        out_copy(q).start()

    @pl.loop(0, chunks)
    def _(q):
        out_copy(q).wait()


def per_device(
    n_ctx, n_head, x_in, bc_in, z_in, dt, log_decay, x_kernel, bc_kernel, x_bias, bc_bias, skip, norm_gain
):
    tokens, channels = x_in.shape
    heads = channels // HEAD_DIM
    chunks = tokens // CHUNK
    height = STATE * channels // PARTS // n_ctx // 128
    share = tokens // n_head
    anywhere, vmem = pl.BlockSpec(memory_space=pl.ANY), pl.BlockSpec(memory_space=pltpu.VMEM)
    dma = pltpu.SemaphoreType.DMA
    a, b, c_part, ent = pl.pallas_call(
        functools.partial(kernel, (n_ctx, n_head, tokens, channels)),
        out_shape=[
            pltpu.VMEM((tokens, channels), F32),
            pltpu.VMEM((tokens, channels), F32),
            pltpu.VMEM((tokens, STATE), BF16),
            pltpu.VMEM((STATE, channels), BF16),
        ],
        in_specs=[anywhere] * 3 + [vmem] * 7,
        out_specs=[vmem] * 4,
        scratch_shapes=[
            pltpu.VMEM((tokens + HALO, channels), BF16),
            pltpu.VMEM((tokens, channels), BF16),
            pltpu.VMEM((chunks, CHUNK + STATE, channels), BF16),
            pltpu.VMEM((tokens, channels), BF16),
            pltpu.VMEM((2 * heads, channels), BF16),
            pltpu.VMEM((24, channels), F32),
            pltpu.VMEM((chunks, CHUNK, 2 * heads), BF16),
            pltpu.VMEM((chunks, CHUNK, 2 * heads), BF16),
            pltpu.VMEM((chunks, CHUNK, 2 * heads), BF16),
            pltpu.VMEM((3 * CHUNK, CHUNK + HALO), BF16),
            pltpu.VMEM((tokens, 2, STATE), BF16),
            pltpu.VMEM((2 * share, STATE), F32),
            pltpu.VMEM((2, n_head, share, STATE), BF16),
            pltpu.VMEM((2, tokens + HALO, STATE), BF16),
            pltpu.VMEM((tokens, STATE), BF16),
            pltpu.VMEM((chunks, STATE, CHUNK), BF16),
            pltpu.VMEM((chunks, CHUNK, CHUNK + STATE), BF16),
            pltpu.VMEM((PARTS, n_ctx, height, 128), BF16),
            pltpu.VMEM((PARTS, n_ctx, height, 128), BF16),
            pltpu.VMEM((PARTS, n_ctx, height, 128), BF16),
            pltpu.VMEM((1, 128), F32),
            pltpu.VMEM((n_ctx, 1, 128), F32),
            pltpu.VMEM((PARTS, n_ctx, 128), F32),
            dma((chunks,)), dma, dma((n_head,)), dma((4,)), dma((2,)), dma((4,)), dma((2,)),
            dma((2 * PARTS,)), dma((2 * PARTS,)),
        ],
        compiler_params=pltpu.CompilerParams(
            collective_id=0, has_side_effects=True, vmem_limit_bytes=45_900_000
        ),
        cost_estimate=pl.CostEstimate(flops=2_500_000_000, bytes_accessed=10_000_000, transcendentals=5_000_000),
    )(x_in, bc_in, z_in, dt.T, log_decay.T, x_kernel, bc_kernel, x_bias[None], bc_bias, skip[None])
    return pl.pallas_call(
        finish,
        out_shape=jax.ShapeDtypeStruct((tokens, channels), BF16),
        in_specs=[vmem] * 5,
        out_specs=anywhere,
        scratch_shapes=[
            pltpu.VMEM((CHUNK, channels), F32),
            pltpu.VMEM((tokens, channels), BF16),
            dma((chunks,)),
        ],
        compiler_params=pltpu.CompilerParams(vmem_limit_bytes=16 * 1024 * 1024),
        cost_estimate=pl.CostEstimate(flops=600_000_000, bytes_accessed=4_000_000, transcendentals=1_000),
    )(a, b, c_part, ent, norm_gain[None])


def solution(mesh):
    placed = (
        P("ctx", "head"),
        P(("ctx", "head"), None, None),
        P("ctx", "head"),
        P("ctx", "head"),
        P("ctx", "head"),
        P(None, "head"),
        P(None, None, "head"),
        P("head"),
        P(None, "head"),
        P("head"),
        P("head"),
    )
    return jax.shard_map(
        functools.partial(per_device, mesh.shape["ctx"], mesh.shape["head"]),
        mesh=mesh, in_specs=placed, out_specs=P("ctx", "head"), check_vma=False,
    )
```

time: 55.4 us -> 49 us (0.88)
  the two profiles are of different devices: /device:TPU:30 before, /device:TPU:1 now
where the time goes in v3:
time: 49 us; the launch traced here: 48.9 us
  Pallas kernels  48.9 us (100%)
    pallas_call x1, Pallas kernels, per_device(): pl.pallas_call(functools.partial(kernel, (n_ctx, n_head, tokens, channels...  45 us
    pallas_call x1, Pallas kernels, per_device(): pl.pallas_call(finish, out_shape=jax.ShapeDtypeStruct((tokens, channels),...  3.9 us

profile of v3, /device:TPU:1, one launch (start us, length us, event | category | flops | bytes accessed | tf_op | source)
XLA Modules:
  0.0 48.9 jit_solution(4705981715201908735)
XLA Ops:
  0.0 0.0 copy-start
  0.0 45.0 %shard_map.109 = (f32[1024,2048]{1,0:T(8,128)S(1)}, f32[1024,2048]{1,0:T(8,128)S(1)}, bf16[1024,128]{1,0:T(8,128)(2,1)S(1)}, bf16[128,2048]{1,0:T(8,128)(2,1)S(1)}) custom-call(bf16[1024,2048]{1,0:T(8,128)(2,1)} %x_hbm.1, bf16[128,2,1024]{2,1,0:T(2,128)(2,1)} %bc_hbm.1, bf16[1024,2048]{1,0:T(8,128)(2,1)} %z_hbm.1, f32[32,1024]{1,0:T(8,128)} %bitcast.6, ...), custom_call_target="tpu_custom_call" | custom-call | flops 2500000000 | bytes 10000000 | tf_op jit(solution)/shard_map/pallas_call | solution.py:421
  45.0 0.0 copy-done
  45.0 3.9 %shard_map.110 = bf16[1024,2048]{1,0:T(8,128)(2,1)} custom-call(f32[1024,2048]{1,0:T(8,128)S(1)} %get-tuple-element.9.a_ref, f32[1024,2048]{1,0:T(8,128)S(1)} %get-tuple-element.10.b_ref, bf16[1024,128]{1,0:T(8,128)(2,1)S(1)} %get-tuple-element.11.c_ref, bf16[128,2048]{1,0:T(8,128)(2,1)S(1)} %get-tuple-element.12.ent_ref, f32[1,2048]{1,0:T(1,128)S(1)} %bitcast.5), custom_call_target="tpu_custom_call" | custom-call | flops 600000000 | bytes 4000000 | tf_op jit(solution)/shard_map/pallas_call | solution.py:463
Async XLA Ops:
  0.0 45.0 %copy-start = (f32[2048]{0:T(1024)S(1)}, f32[2048]{0:T(1024)}, u32[]{:S(2)}) copy-start(f32[2048]{0:T(1024)} %param.21) | copy-start | bytes 24580

commit v4 on v3

--- a/solution.py
+++ b/solution.py
@@ -43,12 +43,13 @@
 
 def kernel(
     sizes,
-    x_hbm, bc_hbm, z_hbm, dt_ref, decay_ref, xk_ref, bck_ref, xb_ref, bcb_ref, skip_ref,
-    a_buf, b_buf, c_buf, ent,
+    x_hbm, bc_hbm, z_hbm, dt_hbm, decay_hbm, xk_hbm, bck_hbm, xb_hbm, bcb_hbm, skip_hbm,
+    a_buf, b_buf, c_buf, ent, square_buf,
+    dt_ref, decay_ref, xk_ref, bck_ref, xb_ref, bcb_ref, skip_ref,
     x_buf, xc_buf, xs_buf, z_buf,
     spread, rows, w_t, g_t, full_t, shift, bc_raw, bc_f32, bc_send, bc_buf, b_conv, b_t, sc_buf,
     f_buf, r_buf, o_buf, d_send, d_buf, e_decay,
-    x_sem, z_sem, raw_sem, bc_sem, hx_sem, hb_sem, d_sem, f_sem, e_sem,
+    small_sem, x_sem, z_sem, raw_sem, bc_sem, hx_sem, hb_sem, d_sem, f_sem, e_sem,
 ):
     n_ctx, n_head, tokens, channels = sizes
     chunks, tiles = tokens // CHUNK, channels // WIDE
@@ -86,14 +87,25 @@
             x_hbm.at[part], x_buf.at[pl.ds(HALO + q * CHUNK, CHUNK)], x_sem.at[q]
         )
 
+    small = [
+        pltpu.make_async_copy(source, target, small_sem.at[i])
+        for i, (source, target) in enumerate((
+            (decay_hbm, decay_ref), (dt_hbm, dt_ref), (skip_hbm, skip_ref), (xk_hbm, xk_ref), (xb_hbm, xb_ref),
+            (bck_hbm, bck_ref), (bcb_hbm, bcb_ref),
+        ))
+    ]
+    small[0].start()
     for t in range(n_head):
         raw_copy(t).start()
+    for copy in small[1:]:
+        copy.start()
     for q in range(chunks):
         x_copy(q).start()
     z_copy = pltpu.make_async_copy(z_hbm, z_buf, z_sem)
     z_copy.start()
 
     d_send[...] = jnp.zeros_like(d_send)
+    small[0].wait()
     sums = lax.dot_general(
         jnp.ones((8, tokens), F32), decay_ref[...], (((1,), (1,)), ((), ())),
         precision=HIGHEST, preferred_element_type=F32,
@@ -111,6 +123,9 @@
     head_of = lax.broadcasted_iota(jnp.int32, (2 * heads, channels), 1) // HEAD_DIM
     row_of = lax.rem(lax.broadcasted_iota(jnp.int32, (2 * heads, channels), 0), heads)
     spread[...] = (head_of == row_of).astype(F32).astype(BF16)
+
+    for copy in small[1:]:
+        copy.wait()
 
     upto = (
         lax.broadcasted_iota(jnp.int32, (CHUNK, CHUNK), 0) <= lax.broadcasted_iota(jnp.int32, (CHUNK, CHUNK), 1)
@@ -150,7 +165,7 @@
         send_sem=hx_sem.at[0], recv_sem=hx_sem.at[1], device_id=(following, h), device_id_type=MESH,
     )
 
-    for which in range(2):
+    def share_out(which):
         @pl.loop(1, n_head)
         def _(d):
             t = lax.rem(h + d, n_head)
@@ -170,9 +185,10 @@
                     device_id=(following, t), device_id_type=MESH,
                 ).start()
 
-        if which == 0:
-            halo_x.start()
         bc_buf[which, mine] = bc_send[which, h]
+
+    share_out(0)
+    halo_x.start()
 
     @pl.loop(1, n_ctx)
     def _(d):
@@ -233,6 +249,7 @@
         return swish_of_twice(half)
 
     arrived(0)
+    share_out(1)
     for q in range(chunks):
         b_part = convolved(0, q)
         b_conv[q * CHUNK : (q + 1) * CHUNK] = b_part.astype(BF16)
@@ -352,9 +369,13 @@
     @pl.loop(0, chunks)
     def _(q):
         part = pl.ds(pl.multiple_of(q * CHUNK, CHUNK), CHUNK)
+        square = jnp.zeros((CHUNK, WIDE), F32)
         for j in range(part_tiles):
             wide = slice(j * WIDE, (j + 1) * WIDE)
-            a_buf[part, wide] = a_buf[part, wide] + b_buf[part, wide] * dot(c_buf[part], ent[:, wide])
+            gated = a_buf[part, wide] + b_buf[part, wide] * dot(c_buf[part], ent[:, wide])
+            a_buf[part, wide] = gated
+            square = square + gated * gated
+        square_buf[part] = square[:, : WIDE // 2] + square[:, WIDE // 2 :]
 
     for p in range(1, PARTS):
         entered(p)
@@ -377,34 +398,35 @@
             pltpu.make_async_copy(sent, sent, sem.at[2 * p]).wait()
 
 
-def finish(a_ref, b_ref, c_ref, ent_ref, gain_ref, out_hbm, g_buf, out_buf, out_sem):
+def finish(a_ref, b_ref, c_ref, ent_ref, square_ref, gain_ref, out_hbm, g_buf, out_buf, out_sem):
     tokens, channels = a_ref.shape
     chunks, tiles = tokens // CHUNK, channels // WIDE
 
     def out_copy(q):
-        part = pl.ds(pl.multiple_of(q * CHUNK, CHUNK), CHUNK)
+        part = pl.ds(q * CHUNK, CHUNK)
         return pltpu.make_async_copy(out_buf.at[part], out_hbm.at[part], out_sem.at[q])
 
-    @pl.loop(0, chunks)
-    def _(q):
-        part = pl.ds(pl.multiple_of(q * CHUNK, CHUNK), CHUNK)
-        square = jnp.zeros((CHUNK, WIDE), F32)
-        for j in range(tiles):
+    first = tiles // PARTS * WIDE
+    for q in range(chunks):
+        part = slice(q * CHUNK, (q + 1) * CHUNK)
+        square = square_ref[part]
+        for j in range(tiles // PARTS, tiles):
             wide = slice(j * WIDE, (j + 1) * WIDE)
-            gated = a_ref[part, wide]
-            if j >= tiles // PARTS:
-                gated = gated + b_ref[part, wide] * dot(c_ref[part], ent_ref[:, wide])
-                g_buf[:, wide] = gated
-            square = square + gated * gated
+            gated = a_ref[part, wide] + b_ref[part, wide] * dot(c_ref[part], ent_ref[:, wide])
+            g_buf[part, wide.start - first : wide.stop - first] = gated
+            squared = gated * gated
+            square = square + squared[:, : WIDE // 2] + squared[:, WIDE // 2 :]
         scale = lax.rsqrt(jnp.sum(square, axis=1, keepdims=True) * (1.0 / channels) + 1e-5)
         for j in range(tiles):
             wide = slice(j * WIDE, (j + 1) * WIDE)
-            gated = a_ref[part, wide] if j < tiles // PARTS else g_buf[:, wide]
+            if j < tiles // PARTS:
+                gated = a_ref[part, wide]
+            else:
+                gated = g_buf[part, wide.start - first : wide.stop - first]
             out_buf[part, wide] = (gated * scale * gain_ref[:, wide]).astype(BF16)
         out_copy(q).start()
 
-    @pl.loop(0, chunks)
-    def _(q):
+    for q in range(chunks):
         out_copy(q).wait()
 
 
@@ -418,17 +440,25 @@
     share = tokens // n_head
     anywhere, vmem = pl.BlockSpec(memory_space=pl.ANY), pl.BlockSpec(memory_space=pltpu.VMEM)
     dma = pltpu.SemaphoreType.DMA
-    a, b, c_part, ent = pl.pallas_call(
+    a, b, c_part, ent, square = pl.pallas_call(
         functools.partial(kernel, (n_ctx, n_head, tokens, channels)),
         out_shape=[
             pltpu.VMEM((tokens, channels), F32),
             pltpu.VMEM((tokens, channels), F32),
             pltpu.VMEM((tokens, STATE), BF16),
             pltpu.VMEM((STATE, channels), BF16),
+            pltpu.VMEM((tokens, WIDE // 2), F32),
         ],
-        in_specs=[anywhere] * 3 + [vmem] * 7,
-        out_specs=[vmem] * 4,
+        in_specs=[anywhere] * 10,
+        out_specs=[vmem] * 5,
         scratch_shapes=[
+            pltpu.VMEM((heads, tokens), F32),
+            pltpu.VMEM((heads, tokens), F32),
+            pltpu.VMEM(x_kernel.shape, F32),
+            pltpu.VMEM(bc_kernel.shape, F32),
+            pltpu.VMEM((1, channels), F32),
+            pltpu.VMEM(bc_bias.shape, F32),
+            pltpu.VMEM((1, heads), F32),
             pltpu.VMEM((tokens + HALO, channels), BF16),
             pltpu.VMEM((tokens, channels), BF16),
             pltpu.VMEM((chunks, CHUNK + STATE, channels), BF16),
@@ -452,27 +482,27 @@
             pltpu.VMEM((1, 128), F32),
             pltpu.VMEM((n_ctx, 1, 128), F32),
             pltpu.VMEM((PARTS, n_ctx, 128), F32),
-            dma((chunks,)), dma, dma((n_head,)), dma((4,)), dma((2,)), dma((4,)), dma((2,)),
+            dma((7,)), dma((chunks,)), dma, dma((n_head,)), dma((4,)), dma((2,)), dma((4,)), dma((2,)),
             dma((2 * PARTS,)), dma((2 * PARTS,)),
         ],
         compiler_params=pltpu.CompilerParams(
-            collective_id=0, has_side_effects=True, vmem_limit_bytes=45_900_000
+            collective_id=0, has_side_effects=True, vmem_limit_bytes=45_370_000
         ),
         cost_estimate=pl.CostEstimate(flops=2_500_000_000, bytes_accessed=10_000_000, transcendentals=5_000_000),
     )(x_in, bc_in, z_in, dt.T, log_decay.T, x_kernel, bc_kernel, x_bias[None], bc_bias, skip[None])
     return pl.pallas_call(
         finish,
         out_shape=jax.ShapeDtypeStruct((tokens, channels), BF16),
-        in_specs=[vmem] * 5,
+        in_specs=[vmem] * 6,
         out_specs=anywhere,
         scratch_shapes=[
-            pltpu.VMEM((CHUNK, channels), F32),
+            pltpu.VMEM((tokens, channels - channels // PARTS), F32),
             pltpu.VMEM((tokens, channels), BF16),
             dma((chunks,)),
         ],
         compiler_params=pltpu.CompilerParams(vmem_limit_bytes=16 * 1024 * 1024),
         cost_estimate=pl.CostEstimate(flops=600_000_000, bytes_accessed=4_000_000, transcendentals=1_000),
-    )(a, b, c_part, ent, norm_gain[None])
+    )(a, b, c_part, ent, square, norm_gain[None])
 
 
 def solution(mesh):

time: 49 us -> 46 us (0.939)
  the two profiles are of different devices: /device:TPU:1 before, /device:TPU:24 now
where the time goes in v4:
time: 46 us; the launch traced here: 45.9 us
  Pallas kernels  45.8 us (100%)
    pallas_call x1, Pallas kernels, per_device(): pl.pallas_call(functools.partial(kernel, (n_ctx, n_head, tokens, channels...  43 us
    pallas_call x1, Pallas kernels, per_device(): pl.pallas_call(finish, out_shape=jax.ShapeDtypeStruct((tokens, channels),...  2.87 us

profile of v4, /device:TPU:24, one launch (start us, length us, event | category | flops | bytes accessed | tf_op | source)
XLA Modules:
  0.0 45.9 jit_solution(7135056217386325920)
XLA Ops:
  0.0 0.0 copy-start
  0.0 43.0 %shard_map.109 = (f32[1024,2048]{1,0:T(8,128)S(1)}, f32[1024,2048]{1,0:T(8,128)S(1)}, bf16[1024,128]{1,0:T(8,128)(2,1)S(1)}, bf16[128,2048]{1,0:T(8,128)(2,1)S(1)}, f32[1024,128]{1,0:T(8,128)S(1)}) custom-call(bf16[1024,2048]{1,0:T(8,128)(2,1)} %x_hbm.1, bf16[128,2,1024]{2,1,0:T(2,128)(2,1)} %bc_hbm.1, bf16[1024,2048]{1,0:T(8,128)(2,1)} %z_hbm.1, ...), custom_call_target="tpu_custom_call" | custom-call | flops 2500000000 | bytes 10000000 | tf_op jit(solution)/shard_map/pallas_call | solution.py:443
  43.0 0.0 copy-done
  43.0 2.9 %shard_map.110 = bf16[1024,2048]{1,0:T(8,128)(2,1)} custom-call(f32[1024,2048]{1,0:T(8,128)S(1)} %get-tuple-element.10.a_ref, f32[1024,2048]{1,0:T(8,128)S(1)} %get-tuple-element.11.b_ref, bf16[1024,128]{1,0:T(8,128)(2,1)S(1)} %get-tuple-element.12.c_ref, bf16[128,2048]{1,0:T(8,128)(2,1)S(1)} %get-tuple-element.13.ent_ref, ...), custom_call_target="tpu_custom_call" | custom-call | flops 600000000 | bytes 4000000 | tf_op jit(solution)/shard_map/pallas_call | solution.py:493
Async XLA Ops:
  0.0 43.0 %copy-start = (f32[2048]{0:T(1024)S(1)}, f32[2048]{0:T(1024)}, u32[]{:S(2)}) copy-start(f32[2048]{0:T(1024)} %param.21) | copy-start | bytes 24580

commit v5 on v4

--- a/solution.py
+++ b/solution.py
@@ -166,8 +166,7 @@
     )
 
     def share_out(which):
-        @pl.loop(1, n_head)
-        def _(d):
+        for d in sorted(range(1, n_head), key=lambda d: (-min(d, n_head - d), d)):
             t = lax.rem(h + d, n_head)
             pltpu.make_async_remote_copy(
                 src_ref=bc_send.at[which, t], dst_ref=bc_buf.at[which, mine],
@@ -343,8 +342,7 @@
             pl.ds(pl.multiple_of(pair(p) * 128, 128), 128),
         )
 
-        @pl.loop(1, n_ctx)
-        def _(d):
+        for d in sorted(range(1, n_ctx), key=lambda d: (-min(d % 8, 8 - d % 8), d)):
             t = lax.rem(c + d, n_ctx)
             pltpu.make_async_remote_copy(
                 src_ref=o_buf.at[p, t], dst_ref=ent.at[place], send_sem=e_sem.at[2 * p], recv_sem=e_sem.at[2 * p + 1],

time: 46 us -> 46.7 us (1.015)
  Pallas kernels: 45.8 us -> 46.6 us
    pallas_call x1, Pallas kernels: 43 us -> 43.8 us  [per_device(): pl.pallas_call(functools.partial(kernel, (n_ctx, n_head, tokens, channels...]
where the time goes in v5:
time: 46.7 us; the launch traced here: 46.6 us
  Pallas kernels  46.6 us (100%)
    pallas_call x1, Pallas kernels, per_device(): pl.pallas_call(functools.partial(kernel, (n_ctx, n_head, tokens, channels...  43.8 us
    pallas_call x1, Pallas kernels, per_device(): pl.pallas_call(finish, out_shape=jax.ShapeDtypeStruct((tokens, channels),...  2.87 us

profile of v5, /device:TPU:24, one launch (start us, length us, event | category | flops | bytes accessed | tf_op | source)
XLA Modules:
  0.0 46.6 jit_solution(5306301630177507293)
XLA Ops:
  0.0 0.0 copy-start
  0.0 43.8 %shard_map.109 = (f32[1024,2048]{1,0:T(8,128)S(1)}, f32[1024,2048]{1,0:T(8,128)S(1)}, bf16[1024,128]{1,0:T(8,128)(2,1)S(1)}, bf16[128,2048]{1,0:T(8,128)(2,1)S(1)}, f32[1024,128]{1,0:T(8,128)S(1)}) custom-call(bf16[1024,2048]{1,0:T(8,128)(2,1)} %x_hbm.1, bf16[128,2,1024]{2,1,0:T(2,128)(2,1)} %bc_hbm.1, bf16[1024,2048]{1,0:T(8,128)(2,1)} %z_hbm.1, ...), custom_call_target="tpu_custom_call" | custom-call | flops 2500000000 | bytes 10000000 | tf_op jit(solution)/shard_map/pallas_call | solution.py:441
  43.8 0.0 copy-done
  43.8 2.9 %shard_map.110 = bf16[1024,2048]{1,0:T(8,128)(2,1)} custom-call(f32[1024,2048]{1,0:T(8,128)S(1)} %get-tuple-element.10.a_ref, f32[1024,2048]{1,0:T(8,128)S(1)} %get-tuple-element.11.b_ref, bf16[1024,128]{1,0:T(8,128)(2,1)S(1)} %get-tuple-element.12.c_ref, bf16[128,2048]{1,0:T(8,128)(2,1)S(1)} %get-tuple-element.13.ent_ref, ...), custom_call_target="tpu_custom_call" | custom-call | flops 600000000 | bytes 4000000 | tf_op jit(solution)/shard_map/pallas_call | solution.py:491
Async XLA Ops:
  0.0 43.8 %copy-start = (f32[2048]{0:T(1024)S(1)}, f32[2048]{0:T(1024)}, u32[]{:S(2)}) copy-start(f32[2048]{0:T(1024)} %param.21) | copy-start | bytes 24580
